TPU v7x, 128 devices: a whole 4x4x4 slice. The times are simulated.
128 devices in a mesh: src: 16 (over x, z_lo, core), tgt: 8 (over y, z_hi).
Axes of the slice: x: 4, y: 4, z: 4 (z_hi: 2, z_lo: 2; z = z_hi * 2 + z_lo), core: 2. Of those that a mesh axis runs over, the one named last changes fastest.
Arguments:
- source_points: float32 [16384, 256], P('src'), may hold values from -24 to 24
- target_points: float32 [32768, 256], P(('tgt', 'src')), may hold values from -24 to 24
- target_potential: float32 [32768], P('tgt'), may hold values from -0.5 to 0.5
Outputs:
- source_potential: float32 [16384], P(('src', 'tgt'))
- target_update: float32 [32768], P(('tgt', 'src'))
- transport_map: float32 [16384, 256], P(('src', 'tgt'))
All inputs are finite; a program needn't handle non-finite values.
Results may differ from a plain program's by a relative error of at most 0.0029.
Values sent between devices are 32-bit elements; how exact they have to be, the bound alone decides.
No kernel may reach another device: no remote copies, remote signals or barrier semaphores. Data moves between devices by JAX's collectives and lax.ppermute only.
A program may use at most 64 MiB of HBM per device.

v0:
```python
import math

import jax
import jax.numpy as jnp
from jax import lax
from jax.sharding import PartitionSpec as P

epsilon = 0.05
precise = lax.Precision.HIGHEST


def pair_cost(points, squares, segment):
    products = lax.dot_general(
        points,
        segment,
        (((1,), (1,)), ((), ())),
        precision=precise,
        preferred_element_type=jnp.float32,
    )
    segment_squares = jnp.sum(segment * segment, axis=1)
    return (squares[:, None] + segment_squares[None, :] - 2.0 * products) / points.shape[1]


def local_sweep(gathered, update, initial):
    length = gathered.shape[0]
    columns = math.gcd(length, 256)

    def advance(position, running):
        offset = position * columns
        segment = lax.dynamic_slice_in_dim(gathered, offset, columns, 0)
        return update(running, segment, offset)

    return lax.fori_loop(0, length // columns, advance, initial)


def shards(source_points, target_points, target_potential):
    src_devices = lax.axis_size("src")
    tgt_devices = lax.axis_size("tgt")
    source_rows = source_points.shape[0]
    target_rows = target_potential.shape[0]
    squares = jnp.sum(source_points * source_points, axis=1)

    def potential_scores(potential, segment, offset):
        window = lax.dynamic_slice_in_dim(potential, offset, segment.shape[0], 0)
        return (window[None, :] - pair_cost(source_points, squares, segment)) / epsilon

    def row_update(running, segment, offset):
        current_top, current_total = running
        scores = potential_scores(target_potential, segment, offset)
        highest = jnp.maximum(current_top, jnp.max(scores, axis=1))
        total = current_total * jnp.exp(current_top - highest) + jnp.sum(
            jnp.exp(scores - highest[:, None]), axis=1
        )
        return (highest, total)

    row_start = (
        jnp.full((source_rows,), -jnp.inf, jnp.float32),
        jnp.zeros((source_rows,), jnp.float32),
    )
    gathered = lax.all_gather(target_points, "src", axis=0, tiled=True)
    row_top, row_total = local_sweep(gathered, row_update, row_start)
    row_high = lax.pmax(row_top, "tgt")
    row_sum = lax.psum(row_total * jnp.exp(row_top - row_high), "tgt")
    source_potential = -epsilon * (
        row_high + jnp.log(row_sum) - math.log(target_rows * tgt_devices)
    )

    def column_update(running, segment, offset):
        column_top, column_total = running
        scores = (source_potential[:, None] - pair_cost(source_points, squares, segment)) / epsilon
        highest = jnp.max(scores, axis=0)
        total = jnp.sum(jnp.exp(scores - highest[None, :]), axis=0)
        return (
            lax.dynamic_update_slice_in_dim(column_top, highest, offset, 0),
            lax.dynamic_update_slice_in_dim(column_total, total, offset, 0),
        )

    column_start = (jnp.zeros((target_rows,), jnp.float32), jnp.zeros((target_rows,), jnp.float32))
    column_top, column_total = local_sweep(gathered, column_update, column_start)
    column_high = lax.pmax(column_top, "src")
    column_sum = lax.psum(column_total * jnp.exp(column_top - column_high), "src")
    target_update = -epsilon * (
        column_high + jnp.log(column_sum) - math.log(source_rows * src_devices)
    )

    def shift_update(running, segment, offset):
        scores = potential_scores(target_update, segment, offset)
        return jnp.maximum(running, jnp.max(scores, axis=1))

    shift_start = jnp.full((source_rows,), -jnp.inf, jnp.float32)
    local_high = local_sweep(gathered, shift_update, shift_start)
    map_high = lax.pmax(local_high, "tgt")

    def value_update(running, segment, offset):
        numerator, denominator = running
        scores = potential_scores(target_update, segment, offset)
        weights = jnp.exp(scores - map_high[:, None])
        denominator = denominator + jnp.sum(weights, axis=1)
        numerator = numerator + jnp.dot(
            weights.astype(jnp.bfloat16),
            segment.astype(jnp.bfloat16),
            preferred_element_type=jnp.float32,
        )
        return (numerator, denominator)

    value_start = (
        jnp.zeros((source_rows, source_points.shape[1]), jnp.float32),
        jnp.zeros((source_rows,), jnp.float32),
    )
    numerator, denominator = local_sweep(gathered, value_update, value_start)
    shared_numerator, shared_denominator = (
        lax.psum_scatter(numerator, "tgt", scatter_dimension=0, tiled=True),
        lax.psum_scatter(denominator, "tgt", scatter_dimension=0, tiled=True),
    )
    transport_map = shared_numerator / shared_denominator[:, None]
    source_share = source_rows // tgt_devices
    own_source = lax.dynamic_slice_in_dim(
        source_potential, lax.axis_index("tgt") * source_share, source_share, 0
    )
    target_share = target_rows // src_devices
    own_target = lax.dynamic_slice_in_dim(
        target_update, lax.axis_index("src") * target_share, target_share, 0
    )
    return (own_source, own_target, transport_map)


def solution(mesh):
    return jax.shard_map(
        shards,
        mesh=mesh,
        in_specs=(P("src", None), P(("tgt", "src"), None), P("tgt")),
        out_specs=(P(("src", "tgt")), P(("tgt", "src")), P(("src", "tgt"), None)),
        check_vma=False,
    )
```

profile of v0, /device:TPU:0, one launch (start us, length us, event | category | flops | bytes accessed | tf_op | source)
XLA Modules:
  0.0 587.7 jit_solution(13407104034994823953)
XLA Ops:
  9.4 40.3 %all-gather.2.cloned.1.call-done = f32[4096,256]{1,0:T(8,128)} async-done(((f32[256,256]{1,0:T(8,128)}), f32[4096,256]{1,0:T(8,128)}) %all-gather.2.cloned.1.call-update) | async-done | bytes 4194320 | tf_op jit(solution)/shard_map/all_gather | solution.py:60
  49.7 74.1 %while.62 = (s32[]{:T(128)}, f32[1024]{0:T(1024)S(1)}, f32[1024]{0:T(1024)S(1)}, f32[4096]{0:T(1024)}, f32[1024]{0:T(1024)S(1)}, /*index=5*/f32[4096,256]{1,0:T(...) while((s32[]{:T(128)}, f32[1024]{0:T(1024)S(1)}, ...), condition=%wide.region_5.0_spmd.clone, body=%wide.region_1.0_spmd.clone.sunk | while | flops 807801600 | bytes 3732666 | solution.py:33
  123.8 23.9 %pmax.21 = f32[1024]{0:T(1024)S(1)} all-reduce(f32[1024]{0:T(1024)S(1)} %get-tuple-element.502), channel_id=1, replica_groups=mesh['src'=16,'tgt'=8] {'tgt'}, use_global_device_ids=true, to_apply=%region_6.0 | all-reduce | flops 1024 | bytes 8192 | tf_op jit(solution)/shard_map/pmax | solution.py:62
  147.7 19.0 %psum.14 = f32[1024]{0:T(1024)S(1)} all-reduce(f32[1024]{0:T(1024)S(1)} %exponential_multiply_fusion.1), channel_id=1, replica_groups=mesh['src'=16,'tgt'=8] {'tgt'}, use_global_device_ids=true, to_apply=%region_7.0 | all-reduce | flops 1024 | bytes 8192 | tf_op jit(solution)/shard_map/psum | solution.py:63
  166.7 72.8 %while.61 = (s32[]{:T(128)}, f32[4096]{0:T(1024)S(1)}, f32[4096]{0:T(1024)S(1)}, f32[1024]{0:T(1024)S(1)}, f32[1024]{0:T(1024)S(1)}, /*index=5*/f32[4096,256]{1,...) while((s32[]{:T(128)}, f32[4096]{0:T(1024)S(1)}, ...), condition=%wide.region_12.0_spmd, body=%wide.region_8.0_spmd.sunk | while | flops 807795968 | bytes 3687595 | solution.py:33
  239.5 52.9 %pmax.22 = f32[4096]{0:T(1024)S(1)} all-reduce(f32[4096]{0:T(1024)S(1)} %get-tuple-element.504), channel_id=1, replica_groups=mesh['src'=16,'tgt'=8] {'src'}, use_global_device_ids=true, to_apply=%region_13.0 | all-reduce | flops 4096 | bytes 32768 | tf_op jit(solution)/shard_map/pmax | solution.py:80
  292.3 52.9 %psum.15 = f32[4096]{0:T(1024)S(1)} all-reduce(f32[4096]{0:T(1024)S(1)} %exponential_multiply_fusion), channel_id=1, replica_groups=mesh['src'=16,'tgt'=8] {'src'}, use_global_device_ids=true, to_apply=%region_14.0 | all-reduce | flops 4096 | bytes 32768 | tf_op jit(solution)/shard_map/psum | solution.py:81
  345.2 59.8 %while.63 = (s32[]{:T(128)}, f32[1024]{0:T(1024)S(1)}, f32[4096]{0:T(1024)S(1)}, f32[1024]{0:T(1024)S(1)}, f32[4096,256]{1,0:T(8,128)}, /*index=5*/f32[1024,256]...) while((s32[]{:T(128)}, f32[1024]{0:T(1024)S(1)}, f32[4096]{0:T(1024)S(1)}, ...), condition=%wide.region_18.0_spmd.clone, body=%wide.region_15.0_spmd.clone.sunk | while | flops 807273216 | bytes 1598641 | solution.py:33
  405.1 22.5 %pmax.23 = f32[1024]{0:T(1024)S(1)} all-reduce(f32[1024]{0:T(1024)S(1)} %get-tuple-element.506), channel_id=1, replica_groups=mesh['src'=16,'tgt'=8] {'tgt'}, use_global_device_ids=true, to_apply=%region_19.0 | all-reduce | flops 1024 | bytes 8192 | tf_op jit(solution)/shard_map/pmax | solution.py:92
  427.6 85.1 %while.64 = (s32[]{:T(128)}, f32[1024,256]{1,0:T(8,128)S(1)}, f32[1024]{0:T(1024)S(1)}, f32[4096]{0:T(1024)S(1)}, f32[1024]{0:T(1024)S(1)}, /*index=5*/f32[4096,...) while((s32[]{:T(128)}, f32[1024,256]{1,0:T(8,128)S(1)}, ...), condition=%wide.region_23.0_spmd.clone, body=%wide.region_20.0_spmd.clone.sunk | while | flops 942539520 | bytes 4879558 | solution.py:33
  428.7 2.7 fusion.63
  434.0 2.7 fusion.63
  439.4 2.7 fusion.63
  444.7 2.7 fusion.63
  450.0 2.7 fusion.63
  455.3 2.7 fusion.63
  460.6 2.7 fusion.63
  471.3 2.7 fusion.63
  492.5 2.7 fusion.63
  497.8 2.7 fusion.63
  503.2 2.7 fusion.63
  508.5 2.7 fusion.63
  516.1 19.0 %all-reduce = f32[1024]{0:T(1024)S(1)} all-reduce(f32[1024]{0:T(1024)S(1)} %get-tuple-element.508), channel_id=3, replica_groups=mesh['src'=16,'tgt'=8] {'tgt'}, use_global_device_ids=true, to_apply=%region_25.0.clone | all-reduce | flops 1024 | bytes 8192
  535.2 44.1 %reduce-scatter.2.cloned.1.call-done = f32[128,256]{1,0:T(8,128)} async-done(((f32[1024,256]{1,0:T(8,128)}), f32[128,256]{1,0:T(8,128)}) %reduce-scatter.2.cloned.1.call-update) | async-done | bytes 131088 | tf_op jit(solution)/shard_map/reduce_scatter | solution.py:112
  (349 shorter events, 263.8 us)
Async XLA Ops:
  7.2 42.5 %all-gather.2.cloned.1.call-start = ((), (), s32[]{:S(2)}) async-start(), calls=%async_computation.1 | async-start | bytes 4456448 | tf_op jit(solution)/shard_map/all_gather | solution.py:60
  7.9 571.3 %reduce-scatter.2.cloned.1.call-start = ((), (), s32[]{:S(2)}) async-start(), calls=%async_computation.2 | async-start | bytes 1179648 | tf_op jit(solution)/shard_map/reduce_scatter | solution.py:112
  427.6 86.1 %copy-start.1 = (u32[128]{0:T(128)S(1)}, u32[128]{0:T(128)}, u32[]{:S(2)}) copy-start(u32[128]{0:T(128)} %constant.271) | copy-start | bytes 1540
  512.6 1.0 copy-start
Sparse Core Ops, SparseCore 0:
  9.7 39.9 all-gather.1
  513.8 65.4 reduce-scatter.1
where the time goes:
time: 593 us; the launch traced here: 588 us
  matrix products  190 us (32%)
  blocking collectives  190 us (32%)
  waiting for transfers between devices  85 us (14%)
  other arithmetic  79.1 us (13%)
  local copies, waits for them, and re-layouts  25.9 us (4%)
  between operations  14.8 us (2%)
    dot_general x64, matrix products, pair_cost(): lax.dot_general(points, segment, (((1,), (1,)), ((), ())), precision=prec...  167 us
    reduce_sum x64, other arithmetic, pair_cost(): segment_squares = jnp.sum(segment * segment, axis=1)  67.9 us
    psum x1, blocking collectives, shards(): lax.psum(column_total * jnp.exp(column_top - column_high), 'src')  52.9 us
    pmax x1, blocking collectives, shards(): column_high = lax.pmax(column_top, 'src')  52.9 us
    reduce_scatter x1, waiting for transfers between devices, shards(): lax.psum_scatter(numerator, 'tgt', scatter_dimension=0, tiled=True)  44.1 us
    all_gather x1, waiting for transfers between devices, shards(): gathered = lax.all_gather(target_points, 'src', axis=0, tiled=True)  40.3 us
    pmax x1, blocking collectives, shards(): row_high = lax.pmax(row_top, 'tgt')  23.9 us
    dot_general x16, matrix products, value_update(): jnp.dot(weights.astype(jnp.bfloat16), segment.astype(jnp.bfloat16), prefe...  22.9 us
  transfers between devices with their start and end apart: 2, of which 2 were waited for; matrix products, arithmetic and copies ran while one was open for 1% of the time, Pallas kernels for 0%

commit v1 on v0

v1 whole, which is shorter than its diff:
```python
import functools
import math

import jax
import jax.numpy as jnp
from jax import lax
from jax.experimental import pallas as pl
from jax.experimental.pallas import tpu as pltpu
from jax.sharding import PartitionSpec as P

epsilon = 0.05
LOG2E = math.log2(math.e)
VMEM = pltpu.VMEM
LIMIT = 40 * 1024 * 1024


def spec():
    return pl.BlockSpec(memory_space=VMEM)


def params():
    return pltpu.CompilerParams(vmem_limit_bytes=LIMIT)


def split_kernel(scale, x_ref, out_ref):
    x = x_ref[...] * scale
    width = x.shape[1]
    high = x.astype(jnp.bfloat16)
    low = (x - high.astype(jnp.float32)).astype(jnp.bfloat16)
    out_ref[:, 0:width] = high
    out_ref[:, width : 2 * width] = high
    out_ref[:, 2 * width : 3 * width] = low


def transposed(block):
    return block.T


def score_kernel(ids, first, last, block, *refs):
    refs = list(refs)
    x_ref, ta_ref, tb_ref, pot_ref = refs[:4]
    refs = refs[4:]
    if not first:
        top_in, total_in = refs[:2]
        refs = refs[2:]
    score_ref, low_ref, top_ref, total_ref = refs[:4]
    piece, width = ta_ref.shape
    me = lax.axis_index("src")
    factor = LOG2E / epsilon
    parts = []
    offsets = []
    for k, t_ref in enumerate((ta_ref, tb_ref)):
        t = t_ref[...]
        low_ref[k * piece : (k + 1) * piece, :] = t.astype(jnp.bfloat16)
        tt = t.T
        high = tt.astype(jnp.bfloat16)
        low = (tt - high.astype(jnp.float32)).astype(jnp.bfloat16)
        parts.append(jnp.concatenate([high, low, high], axis=0))
        squares = jnp.sum(tt * tt, axis=0, keepdims=True)
        potential = pot_ref[pl.ds(ids[k](me), 1), :]
        offsets.append(potential * factor - squares * (factor / width))
    right = jnp.concatenate(parts, axis=1)
    offset = jnp.concatenate(offsets, axis=1)
    rows = x_ref.shape[0]
    columns = right.shape[1]
    for start in range(0, rows, block):
        at = slice(start, start + block)
        score = jnp.dot(x_ref[at, :], right, preferred_element_type=jnp.float32) + offset
        score_ref[at, :] = score
        tiles = [score[:, k : k + 128] for k in range(0, columns, 128)]
        top = functools.reduce(jnp.maximum, tiles)
        if not first:
            old = top_in[at, :]
            top = jnp.maximum(top, old)
        total = sum(jnp.exp2(tile - top) for tile in tiles)
        if not first:
            total = total + total_in[at, :] * jnp.exp2(old - top)
        top_ref[at, :] = top
        total_ref[at, :] = total
    if last:
        row_ref = refs[4]
        for k in range(rows // 128):
            at = slice(k * 128, (k + 1) * 128)
            top = top_ref[at, :].T
            total = total_ref[at, :].T
            highest = jnp.max(top, axis=0, keepdims=True)
            whole = jnp.sum(total * jnp.exp2(top - highest), axis=0, keepdims=True)
            row_ref[k : k + 1, :] = highest + jnp.log2(whole)


def column_kernel(groups, log_targets, *refs):
    score_refs = refs[: len(groups)]
    rows_ref, column_ref, level_ref, add_ref = refs[len(groups) :]
    parts = [rows_ref[k] for k in range(rows_ref.shape[0])]
    highest = functools.reduce(jnp.maximum, parts)
    level = highest + jnp.log2(sum(jnp.exp2(part - highest) for part in parts))
    level_ref[...] = level
    add = log_targets - level
    for k in range(add.shape[0]):
        add_ref[k * 128 : (k + 1) * 128, :] = jnp.broadcast_to(add[k : k + 1, :], (128, 128)).T
    me = lax.axis_index("src")
    rows = add_ref.shape[0]
    step = 128
    for group, score_ref in zip(groups, score_refs, strict=True):
        piece = score_ref.shape[1] // 2
        for k in range(2):
            outs = []
            for c in range(k * piece, (k + 1) * piece, 128):
                top = None
                for r in range(0, rows, step):
                    v = score_ref[r : r + step, c : c + 128] + add_ref[r : r + step, :]
                    v = jnp.max(v.reshape(step // 8, 8, 128), axis=0)
                    top = v if top is None else jnp.maximum(top, v)
                high = jnp.max(top, axis=0, keepdims=True)
                total = None
                for r in range(0, rows, step):
                    v = score_ref[r : r + step, c : c + 128] + add_ref[r : r + step, :]
                    v = jnp.sum(jnp.exp2(v - high).reshape(step // 8, 8, 128), axis=0)
                    total = v if total is None else total + v
                outs.append(high + jnp.log2(jnp.sum(total, axis=0, keepdims=True)))
            column_ref[pl.ds(group[k](me), 1), :] = jnp.concatenate(outs, axis=1)


def map_kernel(groups, block, *refs):
    count = len(groups)
    score_refs = refs[:count]
    low_refs = refs[count : 2 * count]
    add_ref, parts_ref, out_ref, level_ref, sum_ref, weight_ref = refs[2 * count :]
    parts = [parts_ref[k] for k in range(parts_ref.shape[0])]
    highest = functools.reduce(jnp.maximum, parts)
    level_ref[...] = highest + jnp.log2(sum(jnp.exp2(part - highest) for part in parts))
    me = lax.axis_index("src")
    rows = add_ref.shape[0]
    for g, group in enumerate(groups):
        level = jnp.concatenate([level_ref[pl.ds(group[k](me), 1), :] for k in range(2)], axis=1)
        columns = level.shape[1]
        for start in range(0, rows, block):
            at = slice(start, start + block)
            add = add_ref[at, :]
            total = None
            weights = []
            for c in range(0, columns, 128):
                w = jnp.exp2(score_refs[g][at, c : c + 128] + add - level[:, c : c + 128])
                total = w if total is None else total + w
                weights.append(w.astype(jnp.bfloat16))
            part = jnp.dot(
                jnp.concatenate(weights, axis=1), low_refs[g][...], preferred_element_type=jnp.float32
            )
            for r in range(0, block, 128):
                k = (start + r) // 128
                if g == 0:
                    out_ref[k, 0:128, :] = part[r : r + 128, :]
                else:
                    out_ref[k, 0:128, :] += part[r : r + 128, :]
            if g == 0:
                sum_ref[at, :] = total
            else:
                sum_ref[at, :] += total
    for k in range(rows // 128):
        total = jnp.sum(sum_ref[k * 128 : (k + 1) * 128, :].T, axis=0, keepdims=True)
        out_ref[k, 128:136, :] = jnp.broadcast_to(
            jnp.concatenate([total] * (out_ref.shape[2] // 128), axis=1), (8, out_ref.shape[2])
        )


def quotient_kernel(parts_ref, out_ref):
    rows, width = out_ref.shape
    numerator = parts_ref[0, 0:rows, :]
    denominator = parts_ref[0, rows : rows + 8, 0:128]
    for k in range(1, parts_ref.shape[0]):
        numerator = numerator + parts_ref[k, 0:rows, :]
        denominator = denominator + parts_ref[k, rows : rows + 8, 0:128]
    inverse = jnp.broadcast_to(1.0 / denominator[0:1, :], (128, 128)).T
    for c in range(0, width, 128):
        out_ref[:, c : c + 128] = numerator[:, c : c + 128] * inverse


def shards(source_points, target_points, target_potential):
    sources, tgts = lax.axis_size("src"), lax.axis_size("tgt")
    rows, width = source_points.shape
    columns = target_potential.shape[0]
    piece = target_points.shape[0]
    f32, bf16 = jnp.float32, jnp.bfloat16
    me, mine = lax.axis_index("src"), lax.axis_index("tgt")

    def send(value, to):
        return lax.ppermute(value, "src", [(i, to(i)) for i in range(sources)])

    twin = lambda i: i ^ 1
    across = lambda i: i ^ 2
    far = lambda i: i ^ 8
    ahead = lambda i: (i + 4) % sources
    behind = lambda i: (i + sources - 4) % sources

    own = target_points
    z = send(own, across)
    xp = send(own, ahead)
    xm = send(own, behind)
    x2 = send(own, far)
    zp = send(z, ahead)
    zm = send(z, behind)
    z2 = send(x2, across)
    ident = lambda i: i
    arrivals = [
        (own, ident),
        (xp, behind),
        (xm, ahead),
        (z, across),
        (x2, far),
        (zp, lambda i: across(behind(i))),
        (zm, lambda i: across(ahead(i))),
        (z2, lambda i: across(far(i))),
    ]
    groups = [(of, lambda i, of=of: twin(of(i))) for _, of in arrivals]

    def twin_of(value):
        return send(value, twin)

    left = pl.pallas_call(
        functools.partial(split_kernel, 2.0 * LOG2E / (epsilon * width)),
        out_shape=VMEM((rows, 3 * width), bf16),
        in_specs=[spec()],
        out_specs=spec(),
        compiler_params=params(),
        name="split",
    )(source_points)
    pot = target_potential.reshape(sources, piece)
    state = ()
    scores, lows = [], []
    for g, (block, _) in enumerate(arrivals):
        first, last = g == 0, g == len(arrivals) - 1
        outs = [VMEM((rows, 2 * piece), f32), VMEM((2 * piece, width), bf16), VMEM((rows, 128), f32), VMEM((rows, 128), f32)]
        if last:
            outs.append(VMEM((rows // 128, 128), f32))
        result = pl.pallas_call(
            functools.partial(score_kernel, groups[g], first, last, 256),
            out_shape=outs,
            in_specs=[spec()] * (4 + len(state)),
            out_specs=[spec()] * len(outs),
            input_output_aliases={} if first else {4: 2, 5: 3},
            compiler_params=params(),
            cost_estimate=pl.CostEstimate(
                flops=2 * rows * 2 * piece * 3 * width, bytes_accessed=4 * rows * piece, transcendentals=rows * 2 * piece
            ),
            name="score",
        )(left, block, twin_of(block), pot, *state)
        scores.append(result[0])
        lows.append(result[1])
        state = tuple(result[2:4])
    row_level = result[4]
    spread = jnp.broadcast_to(row_level[None], (tgts,) + row_level.shape)
    row_levels = lax.all_to_all(spread, "tgt", 0, 0)
    column_level, level, add = pl.pallas_call(
        functools.partial(column_kernel, groups, math.log2(columns * tgts)),
        out_shape=[VMEM((sources, piece), f32), VMEM((rows // 128, 128), f32), VMEM((rows, 128), f32)],
        in_specs=[spec()] * (len(scores) + 1),
        out_specs=[spec()] * 3,
        compiler_params=params(),
        name="columns",
    )(*scores, row_levels)
    spread = jnp.broadcast_to(column_level[None], (sources,) + column_level.shape)
    column_levels = lax.all_to_all(spread, "src", 0, 0)
    share = rows // tgts
    partial_map, column_whole = pl.pallas_call(
        functools.partial(map_kernel, groups, 256),
        out_shape=[VMEM((tgts, share + 8, width), f32), VMEM((sources, piece), f32)],
        in_specs=[spec()] * (2 * len(scores) + 2),
        out_specs=[spec()] * 2,
        scratch_shapes=[VMEM((rows, 128), f32), VMEM((8, 128), f32)],
        compiler_params=params(),
        name="map",
    )(*scores, *lows, add, column_levels)
    received = lax.all_to_all(partial_map, "tgt", 0, 0)
    transport_map = pl.pallas_call(
        quotient_kernel,
        out_shape=jax.ShapeDtypeStruct((share, width), f32),
        in_specs=[spec()],
        out_specs=spec(),
        compiler_params=params(),
        name="quotient",
    )(received)
    own_rows = lax.dynamic_slice_in_dim(source_points, mine * share, share, 0)
    squares = jnp.sum(own_rows * own_rows, axis=1) / width
    own_level = lax.dynamic_slice_in_dim(level, mine, 1, 0).reshape(share)
    own_source = squares - epsilon * (own_level / LOG2E - math.log(columns * tgts))
    own_column = lax.dynamic_slice_in_dim(column_whole, me, 1, 0).reshape(piece)
    own_potential = lax.dynamic_slice_in_dim(pot, me, 1, 0).reshape(piece)
    own_target = own_potential - epsilon * (own_column / LOG2E - math.log(rows * sources))
    return own_source, own_target, transport_map


def solution(mesh):
    return jax.shard_map(
        shards,
        mesh=mesh,
        in_specs=(P("src", None), P(("tgt", "src"), None), P("tgt")),
        out_specs=(P(("src", "tgt")), P(("tgt", "src")), P(("src", "tgt"), None)),
        check_vma=False,
    )
```

time: 593 us -> 102 us (0.17)
  matrix products: 190 us -> 0 us
  blocking collectives: 190 us -> 26.9 us
  other arithmetic: 79.1 us -> 2.11 us
  waiting for transfers between devices: 85 us -> 20.7 us
  Pallas kernels: 0 us -> 25.6 us
  local copies, waits for them, and re-layouts: 25.9 us -> 4.69 us
  starting transfers between devices: 0.08 us -> 20.8 us
  between operations: 14.8 us -> 0.79 us
    dot_general x80 -> x0, matrix products: 190 us -> none  [the longest x64 167 us: pair_cost(): lax.dot_general(points, segment, (((1,), (1,)), ((), ())), precision=prec...]
    pmax x3 -> x0, blocking collectives: 99.3 us -> none  [the longest x1 52.9 us: shards(): column_high = lax.pmax(column_top, 'src')]
    reduce_sum x97 -> x1, other arithmetic: 77 us -> 1.01 us  [shards(): squares = jnp.sum(own_rows * own_rows, axis=1) / width]
    psum x2 -> x0, blocking collectives: 71.9 us -> none  [the longest x1 52.9 us: shards(): lax.psum(column_total * jnp.exp(column_top - column_high), 'src')]
    reduce_scatter x1 -> x0, waiting for transfers between devices: 44.1 us -> none  [shards(): lax.psum_scatter(numerator, 'tgt', scatter_dimension=0, tiled=True)]
    all_gather x1 -> x0, waiting for transfers between devices: 40.3 us -> none  [shards(): gathered = lax.all_gather(target_points, 'src', axis=0, tiled=True)]
    all_to_all x0 -> x2, blocking collectives: none -> 26.9 us  [the longest x1 15.8 us: shards(): row_levels = lax.all_to_all(spread, 'tgt', 0, 0)]
    pallas_call x0 -> x12, Pallas kernels: none -> 25.6 us  [the longest x8 10.6 us: shards(): pl.pallas_call(functools.partial(score_kernel, groups[g], first, last, 25...]
  transfers between devices with their start and end apart: 2 -> 16, of which waited for: 2 -> 6; matrix products, arithmetic and copies ran while one was open for 1% -> 3% of each run, Pallas kernels for 0% -> 9%
where the time goes in v1:
time: 102 us
  blocking collectives  26.9 us (26%)
  Pallas kernels  25.6 us (25%)
  starting transfers between devices  20.8 us (20%)
  waiting for transfers between devices  20.7 us (20%)
  local copies, waits for them, and re-layouts  4.69 us (5%)
  other arithmetic  2.11 us (2%)
    ppermute x15, starting transfers between devices, send(): return lax.ppermute(value, 'src', [(i, to(i)) for i in range(sources)])  17.2 us
    all_to_all x1, waiting for transfers between devices, shards(): received = lax.all_to_all(partial_map, 'tgt', 0, 0)  15.9 us
    all_to_all x1, blocking collectives, shards(): row_levels = lax.all_to_all(spread, 'tgt', 0, 0)  15.8 us
    all_to_all x1, blocking collectives, shards(): column_levels = lax.all_to_all(spread, 'src', 0, 0)  11.1 us
    pallas_call x8, Pallas kernels, shards(): pl.pallas_call(functools.partial(score_kernel, groups[g], first, last, 25...  10.6 us
    pallas_call x1, Pallas kernels, shards(): pl.pallas_call(functools.partial(map_kernel, groups, 256), out_shape=[VME...  7.88 us
    pallas_call x1, Pallas kernels, shards(): pl.pallas_call(functools.partial(column_kernel, groups, math.log2(columns...  6.09 us
    ppermute x15, waiting for transfers between devices, send(): return lax.ppermute(value, 'src', [(i, to(i)) for i in range(sources)])  4.84 us
  transfers between devices with their start and end apart: 16, of which 6 were waited for; matrix products, arithmetic and copies ran while one was open for 3% of the time, Pallas kernels for 9%

profile of v1, /device:TPU:0, one launch (start us, length us, event | category | flops | bytes accessed | tf_op | source)
XLA Modules:
  0.0 101.6 jit_solution(15873478054534801399)
XLA Ops:
  0.6 1.6 %collective-permute-start.1 = (f32[256,256]{1,0:T(8,128)}, f32[256,256]{1,0:T(8,128)S(1)}, u32[]{:S(2)}, u32[]{:S(2)}) collective-permute-start(f32[256,256]{1,0:T(8,128)} %refs_1_.1), channel_id=1, source_target_pairs={{0,32},{8,40},{16,48},{24,56},{32,64},{40,72},{48,80},{56,88},{64,... | collective-permute-start | bytes 786440 | tf_op jit(solution)/shard_map/ppermute | solution.py:187
  2.3 1.7 %collective-permute-start.3 = (f32[256,256]{1,0:T(8,128)}, f32[256,256]{1,0:T(8,128)S(1)}, u32[]{:S(2)}, u32[]{:S(2)}) collective-permute-start(f32[256,256]{1,0:T(8,128)} %refs_1_.1), channel_id=1, source_target_pairs={{0,96},{8,104},{16,112},{24,120},{32,0},{40,8},{48,16},{56,24},{64... | collective-permute-start | bytes 786440 | tf_op jit(solution)/shard_map/ppermute | solution.py:187
  3.9 2.0 %collective-permute-start.5 = (f32[256,256]{1,0:T(8,128)}, f32[256,256]{1,0:T(8,128)S(1)}, u32[]{:S(2)}, u32[]{:S(2)}) collective-permute-start(f32[256,256]{1,0:T(8,128)} %refs_1_.1), channel_id=1, source_target_pairs={{0,16},{8,24},{16,0},{24,8},{32,48},{40,56},{48,32},{56,40},{64,80... | collective-permute-start | bytes 786440 | tf_op jit(solution)/shard_map/ppermute | solution.py:187
  5.9 1.8 %collective-permute-start.7 = (f32[256,256]{1,0:T(8,128)}, f32[256,256]{1,0:T(8,128)S(1)}, u32[]{:S(2)}, u32[]{:S(2)}) collective-permute-start(f32[256,256]{1,0:T(8,128)} %refs_1_.1), channel_id=1, source_target_pairs={{0,64},{8,72},{16,80},{24,88},{32,96},{40,104},{48,112},{56,120},{... | collective-permute-start | bytes 786440 | tf_op jit(solution)/shard_map/ppermute | solution.py:187
  7.8 2.3 %collective-permute-done.1.refs_1_ = f32[256,256]{1,0:T(8,128)S(1)} collective-permute-done((f32[256,256]{1,0:T(8,128)}, f32[256,256]{1,0:T(8,128)S(1)}, u32[]{:S(2)}, u32[]{:S(2)}) %collective-permute-start.1) | collective-permute-done | bytes 262176 | tf_op jit(solution)/shard_map/ppermute | solution.py:187
  12.4 6.0 %collective-permute-start.11 = (f32[256,256]{1,0:T(8,128)S(1)}, f32[256,256]{1,0:T(8,128)S(1)}, u32[]{:S(2)}, u32[]{:S(2)}) collective-permute-start(f32[256,256]{1,0:T(8,128)S(1)} %collective-permute-done.5.refs_1_), channel_id=1, source_target_pairs={{0,96},{8,104},{16,112},{24,120},{32,0},{40,8},{48,16},{56,24},{64... | collective-permute-start | bytes 786440 | tf_op jit(solution)/shard_map/ppermute | solution.py:187
  18.4 2.5 %collective-permute-start.13 = (f32[256,256]{1,0:T(8,128)S(1)}, f32[256,256]{1,0:T(8,128)S(1)}, u32[]{:S(2)}, u32[]{:S(2)}) collective-permute-start(f32[256,256]{1,0:T(8,128)S(1)} %collective-permute-done.7.refs_1_), channel_id=1, source_target_pairs={{0,16},{8,24},{16,0},{24,8},{32,48},{40,56},{48,32},{56,40},{64,80... | collective-permute-start | bytes 786440 | tf_op jit(solution)/shard_map/ppermute | solution.py:187
  21.6 1.2 %copy-done.3 = f32[1024,256]{1,0:T(8,128)S(1)} copy-done((f32[1024,256]{1,0:T(8,128)S(1)}, f32[1024,256]{1,0:T(8,128)}, u32[]{:S(2)}) %copy-start.3) | copy-done | bytes 1048600
  23.7 1.2 %score.8 = (f32[1024,512]{1,0:T(8,128)S(1)}, bf16[512,256]{1,0:T(8,128)(2,1)S(1)}, f32[1024,128]{1,0:T(8,128)S(1)}, f32[1024,128]{1,0:T(8,128)S(1)}) custom-call(bf16[1024,768]{1,0:T(8,128)(2,1)S(1)} %split.1.refs_0_, f32[256,256]{1,0:T(8,128)S(1)} %copy-done.4, f32[256,256]{1,0:T(8,128)S(1)} %collective-permute-done.refs_2_, f32[16,256]{1,0:T(8,128)S(1)} %reshape.27.refs_3_), custom_call_target="tpu_custom_call" | custom-call | flops 805306368 | bytes 1048576 | tf_op jit(solution)/shard_map/score/pallas_call | solution.py:235
  25.5 1.3 %score.9 = (f32[1024,512]{1,0:T(8,128)S(1)}, bf16[512,256]{1,0:T(8,128)(2,1)S(1)}, f32[1024,128]{1,0:T(8,128)S(1)}, f32[1024,128]{1,0:T(8,128)S(1)}) custom-call(bf16[1024,768]{1,0:T(8,128)(2,1)S(1)} %split.1.refs_0_, f32[256,256]{1,0:T(8,128)S(1)} %collective-permute-done.1.refs_1_, ...), custom_call_target="tpu_custom_call", output_to_operand_aliasing={{2}: (4, {}), {3}: (5, {})} | custom-call | flops 805306368 | bytes 1048576 | tf_op jit(solution)/shard_map/score/pallas_call | solution.py:235
  27.5 1.3 %score.10 = (f32[1024,512]{1,0:T(8,128)S(1)}, bf16[512,256]{1,0:T(8,128)(2,1)S(1)}, f32[1024,128]{1,0:T(8,128)S(1)}, f32[1024,128]{1,0:T(8,128)S(1)}) custom-call(bf16[1024,768]{1,0:T(8,128)(2,1)S(1)} %split.1.refs_0_, f32[256,256]{1,0:T(8,128)S(1)} %collective-permute-done.3.refs_1_, ...), custom_call_target="tpu_custom_call", output_to_operand_aliasing={{2}: (4, {}), {3}: (5, {})} | custom-call | flops 805306368 | bytes 1048576 | tf_op jit(solution)/shard_map/score/pallas_call | solution.py:235
  28.9 1.3 %score.11 = (f32[1024,512]{1,0:T(8,128)S(1)}, bf16[512,256]{1,0:T(8,128)(2,1)S(1)}, f32[1024,128]{1,0:T(8,128)S(1)}, f32[1024,128]{1,0:T(8,128)S(1)}) custom-call(bf16[1024,768]{1,0:T(8,128)(2,1)S(1)} %split.1.refs_0_, f32[256,256]{1,0:T(8,128)S(1)} %collective-permute-done.5.refs_1_, ...), custom_call_target="tpu_custom_call", output_to_operand_aliasing={{2}: (4, {}), {3}: (5, {})} | custom-call | flops 805306368 | bytes 1048576 | tf_op jit(solution)/shard_map/score/pallas_call | solution.py:235
  30.2 1.3 %score.12 = (f32[1024,512]{1,0:T(8,128)S(1)}, bf16[512,256]{1,0:T(8,128)(2,1)S(1)}, f32[1024,128]{1,0:T(8,128)S(1)}, f32[1024,128]{1,0:T(8,128)S(1)}) custom-call(bf16[1024,768]{1,0:T(8,128)(2,1)S(1)} %split.1.refs_0_, f32[256,256]{1,0:T(8,128)S(1)} %collective-permute-done.7.refs_1_, ...), custom_call_target="tpu_custom_call", output_to_operand_aliasing={{2}: (4, {}), {3}: (5, {})} | custom-call | flops 805306368 | bytes 1048576 | tf_op jit(solution)/shard_map/score/pallas_call | solution.py:235
  31.6 1.3 %score.13 = (f32[1024,512]{1,0:T(8,128)S(1)}, bf16[512,256]{1,0:T(8,128)(2,1)S(1)}, f32[1024,128]{1,0:T(8,128)S(1)}, f32[1024,128]{1,0:T(8,128)S(1)}) custom-call(bf16[1024,768]{1,0:T(8,128)(2,1)S(1)} %split.1.refs_0_, f32[256,256]{1,0:T(8,128)S(1)} %collective-permute-done.9.refs_1_, ...), custom_call_target="tpu_custom_call", output_to_operand_aliasing={{2}: (4, {}), {3}: (5, {})} | custom-call | flops 805306368 | bytes 1048576 | tf_op jit(solution)/shard_map/score/pallas_call | solution.py:235
  32.9 1.3 %score.14 = (f32[1024,512]{1,0:T(8,128)S(1)}, bf16[512,256]{1,0:T(8,128)(2,1)S(1)}, f32[1024,128]{1,0:T(8,128)S(1)}, f32[1024,128]{1,0:T(8,128)S(1)}) custom-call(bf16[1024,768]{1,0:T(8,128)(2,1)S(1)} %split.1.refs_0_, f32[256,256]{1,0:T(8,128)S(1)} %collective-permute-done.11.refs_1_, ...), custom_call_target="tpu_custom_call", output_to_operand_aliasing={{2}: (4, {}), {3}: (5, {})} | custom-call | flops 805306368 | bytes 1048576 | tf_op jit(solution)/shard_map/score/pallas_call | solution.py:235
  34.3 1.3 %copy-done.1 = f32[1024,512]{1,0:T(8,128)} copy-done((f32[1024,512]{1,0:T(8,128)}, f32[1024,512]{1,0:T(8,128)S(1)}, u32[]{:S(2)}) %copy-start.1) | copy-done | bytes 2097176
  35.6 1.4 %score.15 = (f32[1024,512]{1,0:T(8,128)S(1)}, bf16[512,256]{1,0:T(8,128)(2,1)S(1)}, f32[1024,128]{1,0:T(8,128)S(1)}, f32[1024,128]{1,0:T(8,128)S(1)}, f32[8,128]{1,0:T(8,128)S(1)}) custom-call(bf16[1024,768]{1,0:T(8,128)(2,1)S(1)} %split.1.refs_0_, f32[256,256]{1,0:T(8,128)S(1)} %collective-permute-done.13.refs_1_, ...), custom_call_target="tpu_custom_call", output_to_operand_aliasing={{2}: (4, {}), {3}: (5, {})} | custom-call | flops 805306368 | bytes 1048576 | tf_op jit(solution)/shard_map/score/pallas_call | solution.py:235
  37.0 1.3 %copy-done.2 = f32[1024,512]{1,0:T(8,128)} copy-done((f32[1024,512]{1,0:T(8,128)}, f32[1024,512]{1,0:T(8,128)S(1)}, u32[]{:S(2)}) %copy-start.2) | copy-done | bytes 2097176
  38.4 15.8 %all_to_all.15.refs_8_ = f32[8,8,128]{2,1,0:T(8,128)S(1)} all-to-all(f32[8,8,128]{2,1,0:T(8,128)S(1)} %broadcast_in_dim.4), channel_id=1, replica_groups=mesh['src'=16,'tgt'=8] {'tgt'}, dimensions={0} | all-to-all | bytes 65536 | tf_op jit(solution)/shard_map/all_to_all | solution.py:252
  54.1 6.1 %columns.1 = (f32[16,256]{1,0:T(8,128)S(1)}, f32[8,128]{1,0:T(8,128)S(1)}, f32[1024,128]{1,0:T(8,128)S(1)}) custom-call(f32[1024,512]{1,0:T(8,128)S(1)} %get-tuple-element.39.refs_0_, f32[1024,512]{1,0:T(8,128)S(1)} %get-tuple-element.42.refs_1_, f32[1024,512]{1,0:T(8,128)S(1)} %get-tuple-element.45.refs_2_, f32[1024,512]{1,0:T(8,128)S(1)} %get-tuple-element.48.refs_3_, ...), custom_call_target="tpu_custom_call" | custom-call | tf_op jit(solution)/shard_map/columns/pallas_call | solution.py:253
  60.3 11.1 %all_to_all.16.refs_17_ = f32[16,16,256]{2,1,0:T(8,128)S(1)} all-to-all(f32[16,16,256]{2,1,0:T(8,128)S(1)} %broadcast_in_dim.5), channel_id=1, replica_groups=mesh['src'=16,'tgt'=8] {'src'}, dimensions={0} | all-to-all | bytes 524288 | tf_op jit(solution)/shard_map/all_to_all | solution.py:262
  71.4 7.9 %map.1 = (f32[8,136,256]{2,1,0:T(8,128)}, f32[16,256]{1,0:T(8,128)S(1)}) custom-call(f32[1024,512]{1,0:T(8,128)S(1)} %get-tuple-element.39.refs_0_, f32[1024,512]{1,0:T(8,128)S(1)} %get-tuple-element.42.refs_1_, f32[1024,512]{1,0:T(8,128)S(1)} %get-tuple-element.45.refs_2_, f32[1024,512]{1,0:T(8,128)S(1)} %get-tuple-element.48.refs_3_, ...), custom_call_target="tpu_custom_call" | custom-call | tf_op jit(solution)/shard_map/map/pallas_call | solution.py:264
  79.2 3.6 %all-to-all-start.2 = ((f32[8,136,256]{2,1,0:T(8,128)}), f32[8,136,256]{2,1,0:T(8,128)S(1)}, u32[]{:S(2)}, u32[]{:S(2)}) async-start(f32[8,136,256]{2,1,0:T(8,128)} %get-tuple-element.74), calls=%async_computation.2 | async-start | bytes 2228224 | tf_op jit(solution)/shard_map/all_to_all | solution.py:273
  84.9 15.9 %all-to-all-done.2.parts_ref = f32[8,136,256]{2,1,0:T(8,128)S(1)} async-done(((f32[8,136,256]{2,1,0:T(8,128)}), f32[8,136,256]{2,1,0:T(8,128)S(1)}, u32[]{:S(2)}, u32[]{:S(2)}) %all-to-all-start.2) | async-done | bytes 1114144 | tf_op jit(solution)/shard_map/all_to_all | solution.py:273
  (38 shorter events, 8.2 us)
Async XLA Ops:
  0.6 9.4 %collective-permute-start.1 = (f32[256,256]{1,0:T(8,128)}, f32[256,256]{1,0:T(8,128)S(1)}, u32[]{:S(2)}, u32[]{:S(2)}) collective-permute-start(f32[256,256]{1,0:T(8,128)} %refs_1_.1), channel_id=1, source_target_pairs={{0,32},{8,40},{16,48},{24,56},{32,64},{40,72},{48,80},{56,88},{64,... | collective-permute-start | bytes 786440 | tf_op jit(solution)/shard_map/ppermute | solution.py:187
  2.3 8.5 %collective-permute-start.3 = (f32[256,256]{1,0:T(8,128)}, f32[256,256]{1,0:T(8,128)S(1)}, u32[]{:S(2)}, u32[]{:S(2)}) collective-permute-start(f32[256,256]{1,0:T(8,128)} %refs_1_.1), channel_id=1, source_target_pairs={{0,96},{8,104},{16,112},{24,120},{32,0},{40,8},{48,16},{56,24},{64... | collective-permute-start | bytes 786440 | tf_op jit(solution)/shard_map/ppermute | solution.py:187
  3.9 8.0 %collective-permute-start.5 = (f32[256,256]{1,0:T(8,128)}, f32[256,256]{1,0:T(8,128)S(1)}, u32[]{:S(2)}, u32[]{:S(2)}) collective-permute-start(f32[256,256]{1,0:T(8,128)} %refs_1_.1), channel_id=1, source_target_pairs={{0,16},{8,24},{16,0},{24,8},{32,48},{40,56},{48,32},{56,40},{64,80... | collective-permute-start | bytes 786440 | tf_op jit(solution)/shard_map/ppermute | solution.py:187
  5.9 6.4 %collective-permute-start = (f32[256,256]{1,0:T(8,128)}, f32[256,256]{1,0:T(8,128)S(1)}, u32[]{:S(2)}, u32[]{:S(2)}) collective-permute-start(f32[256,256]{1,0:T(8,128)} %refs_1_.1), channel_id=1, source_target_pairs={{0,8},{8,0},{16,24},{24,16},{32,40},{40,32},{48,56},{56,48},{64,72... | collective-permute-start | bytes 786440 | tf_op jit(solution)/shard_map/ppermute | solution.py:187
  5.9 12.4 %collective-permute-start.7 = (f32[256,256]{1,0:T(8,128)}, f32[256,256]{1,0:T(8,128)S(1)}, u32[]{:S(2)}, u32[]{:S(2)}) collective-permute-start(f32[256,256]{1,0:T(8,128)} %refs_1_.1), channel_id=1, source_target_pairs={{0,64},{8,72},{16,80},{24,88},{32,96},{40,104},{48,112},{56,120},{... | collective-permute-start | bytes 786440 | tf_op jit(solution)/shard_map/ppermute | solution.py:187
  10.1 10.8 %collective-permute-start.2 = (f32[256,256]{1,0:T(8,128)S(1)}, f32[256,256]{1,0:T(8,128)S(1)}, u32[]{:S(2)}, u32[]{:S(2)}) collective-permute-start(f32[256,256]{1,0:T(8,128)S(1)} %collective-permute-done.1.refs_1_), channel_id=1, source_target_pairs={{0,8},{8,0},{16,24},{24,16},{32,40},{40,32},{48,56},{56,48},{64,72... | collective-permute-start | bytes 786440 | tf_op jit(solution)/shard_map/ppermute | solution.py:187
  10.8 12.3 %collective-permute-start.4 = (f32[256,256]{1,0:T(8,128)S(1)}, f32[256,256]{1,0:T(8,128)S(1)}, u32[]{:S(2)}, u32[]{:S(2)}) collective-permute-start(f32[256,256]{1,0:T(8,128)S(1)} %collective-permute-done.3.refs_1_), channel_id=1, source_target_pairs={{0,8},{8,0},{16,24},{24,16},{32,40},{40,32},{48,56},{56,48},{64,72... | collective-permute-start | bytes 786440 | tf_op jit(solution)/shard_map/ppermute | solution.py:187
  11.9 13.3 %collective-permute-start.9 = (f32[256,256]{1,0:T(8,128)S(1)}, f32[256,256]{1,0:T(8,128)S(1)}, u32[]{:S(2)}, u32[]{:S(2)}) collective-permute-start(f32[256,256]{1,0:T(8,128)S(1)} %collective-permute-done.5.refs_1_), channel_id=1, source_target_pairs={{0,32},{8,40},{16,48},{24,56},{32,64},{40,72},{48,80},{56,88},{64,... | collective-permute-start | bytes 786440 | tf_op jit(solution)/shard_map/ppermute | solution.py:187
  12.4 14.5 %collective-permute-start.11 = (f32[256,256]{1,0:T(8,128)S(1)}, f32[256,256]{1,0:T(8,128)S(1)}, u32[]{:S(2)}, u32[]{:S(2)}) collective-permute-start(f32[256,256]{1,0:T(8,128)S(1)} %collective-permute-done.5.refs_1_), channel_id=1, source_target_pairs={{0,96},{8,104},{16,112},{24,120},{32,0},{40,8},{48,16},{56,24},{64... | collective-permute-start | bytes 786440 | tf_op jit(solution)/shard_map/ppermute | solution.py:187
  18.4 9.2 %collective-permute-start.13 = (f32[256,256]{1,0:T(8,128)S(1)}, f32[256,256]{1,0:T(8,128)S(1)}, u32[]{:S(2)}, u32[]{:S(2)}) collective-permute-start(f32[256,256]{1,0:T(8,128)S(1)} %collective-permute-done.7.refs_1_), channel_id=1, source_target_pairs={{0,16},{8,24},{16,0},{24,8},{32,48},{40,56},{48,32},{56,40},{64,80... | collective-permute-start | bytes 786440 | tf_op jit(solution)/shard_map/ppermute | solution.py:187
  20.8 8.0 %collective-permute-start.6 = (f32[256,256]{1,0:T(8,128)S(1)}, f32[256,256]{1,0:T(8,128)S(1)}, u32[]{:S(2)}, u32[]{:S(2)}) collective-permute-start(f32[256,256]{1,0:T(8,128)S(1)} %collective-permute-done.5.refs_1_), channel_id=1, source_target_pairs={{0,8},{8,0},{16,24},{24,16},{32,40},{40,32},{48,56},{56,48},{64,72... | collective-permute-start | bytes 786440 | tf_op jit(solution)/shard_map/ppermute | solution.py:187
  21.6 1.2 %copy-start.3 = (f32[1024,256]{1,0:T(8,128)S(1)}, f32[1024,256]{1,0:T(8,128)}, u32[]{:S(2)}) copy-start(f32[1024,256]{1,0:T(8,128)} %x_ref.1) | copy-start | bytes 3145732
  22.8 0.9 copy-start.4
  23.1 7.1 %collective-permute-start.8 = (f32[256,256]{1,0:T(8,128)S(1)}, f32[256,256]{1,0:T(8,128)S(1)}, u32[]{:S(2)}, u32[]{:S(2)}) collective-permute-start(f32[256,256]{1,0:T(8,128)S(1)} %collective-permute-done.7.refs_1_), channel_id=1, source_target_pairs={{0,8},{8,0},{16,24},{24,16},{32,40},{40,32},{48,56},{56,48},{64,72... | collective-permute-start | bytes 786440 | tf_op jit(solution)/shard_map/ppermute | solution.py:187
  25.3 6.3 %collective-permute-start.10 = (f32[256,256]{1,0:T(8,128)S(1)}, f32[256,256]{1,0:T(8,128)S(1)}, u32[]{:S(2)}, u32[]{:S(2)}) collective-permute-start(f32[256,256]{1,0:T(8,128)S(1)} %collective-permute-done.9.refs_1_), channel_id=1, source_target_pairs={{0,8},{8,0},{16,24},{24,16},{32,40},{40,32},{48,56},{56,48},{64,72... | collective-permute-start | bytes 786440 | tf_op jit(solution)/shard_map/ppermute | solution.py:187
  26.9 6.0 %collective-permute-start.12 = (f32[256,256]{1,0:T(8,128)S(1)}, f32[256,256]{1,0:T(8,128)S(1)}, u32[]{:S(2)}, u32[]{:S(2)}) collective-permute-start(f32[256,256]{1,0:T(8,128)S(1)} %collective-permute-done.11.refs_1_), channel_id=1, source_target_pairs={{0,8},{8,0},{16,24},{24,16},{32,40},{40,32},{48,56},{56,48},{64,72... | collective-permute-start | bytes 786440 | tf_op jit(solution)/shard_map/ppermute | solution.py:187
  27.5 8.1 %collective-permute-start.14 = (f32[256,256]{1,0:T(8,128)S(1)}, f32[256,256]{1,0:T(8,128)S(1)}, u32[]{:S(2)}, u32[]{:S(2)}) collective-permute-start(f32[256,256]{1,0:T(8,128)S(1)} %collective-permute-done.13.refs_1_), channel_id=1, source_target_pairs={{0,8},{8,0},{16,24},{24,16},{32,40},{40,32},{48,56},{56,48},{64,72... | collective-permute-start | bytes 786440 | tf_op jit(solution)/shard_map/ppermute | solution.py:187
  32.9 21.2 %copy-start = (f32[1024,512]{1,0:T(8,128)}, f32[1024,512]{1,0:T(8,128)S(1)}, u32[]{:S(2)}) copy-start(f32[1024,512]{1,0:T(8,128)S(1)} %get-tuple-element.54.refs_5_) | copy-start | bytes 6291460
  34.2 1.3 %copy-start.1 = (f32[1024,512]{1,0:T(8,128)}, f32[1024,512]{1,0:T(8,128)S(1)}, u32[]{:S(2)}) copy-start(f32[1024,512]{1,0:T(8,128)S(1)} %get-tuple-element.57.refs_6_) | copy-start | bytes 6291460
  37.0 1.3 %copy-start.2 = (f32[1024,512]{1,0:T(8,128)}, f32[1024,512]{1,0:T(8,128)S(1)}, u32[]{:S(2)}) copy-start(f32[1024,512]{1,0:T(8,128)S(1)} %get-tuple-element.60.refs_7_) | copy-start | bytes 6291460
  79.2 21.6 %all-to-all-start.2 = ((f32[8,136,256]{2,1,0:T(8,128)}), f32[8,136,256]{2,1,0:T(8,128)S(1)}, u32[]{:S(2)}, u32[]{:S(2)}) async-start(f32[8,136,256]{2,1,0:T(8,128)} %get-tuple-element.74), calls=%async_computation.2 | async-start | bytes 2228224 | tf_op jit(solution)/shard_map/all_to_all | solution.py:273

commit v2 on v0

v2 whole, which is shorter than its diff:
```python
import functools
import math

import jax
import jax.numpy as jnp
from jax import lax
from jax.experimental import pallas as pl
from jax.experimental.pallas import tpu as pltpu
from jax.sharding import Mesh
from jax.sharding import PartitionSpec as P

epsilon = 0.05
LOG2E = math.log2(math.e)
VMEM = pltpu.VMEM
LIMIT = 18 * 1024 * 1024


def spec():
    return pl.BlockSpec(memory_space=VMEM)


def params():
    return pltpu.CompilerParams(vmem_limit_bytes=LIMIT)


def split_kernel(scale, own, x_ref, out_ref, *square_ref):
    x = x_ref[...]
    width = x.shape[1]
    if own:
        mine = lax.axis_index("y") * lax.axis_size("zh") + lax.axis_index("zh")
        some = x_ref[pl.ds(pl.multiple_of(mine * 128, 128), 128), :]
        square_ref[0][...] = jnp.sum((some * some).T, axis=0, keepdims=True)
    x = x * scale
    high = x.astype(jnp.bfloat16)
    low = (x - high.astype(jnp.float32)).astype(jnp.bfloat16)
    out_ref[:, 0:width] = high
    out_ref[:, width : 2 * width] = high
    out_ref[:, 2 * width : 3 * width] = low


def place(of):
    return lax.rem(lax.axis_index("x") + of[0], lax.axis_size("x"))


def half_of(of):
    half = lax.axis_index("zl")
    return 1 - half if of[1] else half


def piece_of(of):
    return (place(of) * 2 + half_of(of)) * 2 + lax.axis_index("c")


def column_of(of):
    return place(of) * 2 + half_of(of)


def potential_of(pot_ref, of, piece):
    lines = piece // 128
    start = piece_of(of) * lines
    return jnp.concatenate([pot_ref[pl.ds(start + k, 1), :] for k in range(lines)], axis=1)


def score_rows(x_ref, right_ref, offset_ref, old, score_ref, top_ref, total_ref, block):
    rows, columns = score_ref.shape
    for start in range(0, rows, block):
        at = slice(start, start + block)
        score = jnp.dot(x_ref[at, :], right_ref[...], preferred_element_type=jnp.float32)
        score = score + offset_ref[0:1, :]
        score_ref[at, :] = score
        tiles = [score[:, k : k + 128] for k in range(0, columns, 128)]
        top = functools.reduce(jnp.maximum, tiles)
        if old is not None:
            before = old[0][at, :]
            top = jnp.maximum(top, before)
        total = sum(jnp.exp2(tile - top) for tile in tiles)
        if old is not None:
            total = total + old[1][at, :] * jnp.exp2(before - top)
        top_ref[at, :] = top
        total_ref[at, :] = total


def score_kernel(group, first, last, *refs):
    left_refs, t_refs, pot_refs, refs = refs[:2], refs[2:4], refs[4:6], refs[6:]
    old = (None, None)
    if not first:
        old, refs = (refs[0:2], refs[2:4]), refs[4:]
    score_refs, low_ref, state_refs, refs = refs[:2], refs[2], (refs[3:5], refs[5:7]), refs[7:]
    right_ref, offset_ref = refs[-2:]
    piece, width = t_refs[0].shape
    factor = LOG2E / epsilon
    for k, of in enumerate(group):
        at = slice(k * piece, (k + 1) * piece)
        t = t_refs[k][...]
        low_ref[at, :] = t.astype(jnp.bfloat16)
        tt = t.T
        high = tt.astype(jnp.bfloat16)
        low = (tt - high.astype(jnp.float32)).astype(jnp.bfloat16)
        right_ref[0:width, at] = high
        right_ref[width : 2 * width, at] = low
        right_ref[2 * width : 3 * width, at] = high
        squares = jnp.sum(tt * tt, axis=0, keepdims=True)
        potential = potential_of(pot_refs[int(of[1])], of, piece)
        offset_ref[0:1, at] = potential * factor - squares * (factor / width)
    for side in range(2):
        score_rows(left_refs[side], right_ref, offset_ref, old[side], score_refs[side], *state_refs[side], 256)
        if last:
            top_ref, total_ref = state_refs[side]
            for k in range(top_ref.shape[0] // 128):
                at = slice(k * 128, (k + 1) * 128)
                top = top_ref[at, :].T
                total = total_ref[at, :].T
                highest = jnp.max(top, axis=0, keepdims=True)
                whole = jnp.sum(total * jnp.exp2(top - highest), axis=0, keepdims=True)
                refs[0][side, k : k + 1, :] = highest + jnp.log2(whole)


def log_sum(parts):
    highest = functools.reduce(jnp.maximum, parts)
    return highest + jnp.log2(sum(jnp.exp2(part - highest) for part in parts))


def column_kernel(groups, log_targets, width, *refs):
    count = len(groups)
    score_refs = (refs[:count], refs[count : 2 * count])
    rows_ref, square_ref, column_ref, own_ref = refs[2 * count : 2 * count + 4]
    add_refs = refs[2 * count + 4 :]
    half = lax.axis_index("c")
    group = rows_ref.shape[0] // 2
    mine = lax.axis_index("y") * lax.axis_size("zh") + lax.axis_index("zh")
    for side in range(2):
        parts = [rows_ref[half * group + k, side] for k in range(group)]
        parts += [rows_ref[(1 - half) * group + k, 1 - side] for k in range(group)]
        add = log_targets - log_sum(parts)
        for k in range(add.shape[0]):
            add_refs[side][k * 128 : (k + 1) * 128, :] = jnp.broadcast_to(add[k : k + 1, :], (128, 128)).T
        if side == 0:
            chosen = jnp.where(lax.broadcasted_iota(jnp.int32, add.shape, 0) == mine, add, 0.0)
            chosen = jnp.sum(chosen, axis=0, keepdims=True)
            own_ref[...] = square_ref[...] / width + chosen * (epsilon / LOG2E)
    rows = add_refs[0].shape[0]
    step = 64
    columns = score_refs[0][0].shape[1]
    tiles = [(g, slice(c, c + 128)) for g in range(count) for c in range(0, columns, 128)]

    def sweep(side):
        def one(n, sums):
            at = pl.ds(pl.multiple_of(n * step, step), step)
            add = add_refs[side][at, :]
            out = []
            for (g, c), total in zip(tiles, sums, strict=True):
                v = jnp.exp2(score_refs[side][g][at, c] + add)
                out.append(total + jnp.sum(v.reshape(step // 8, 8, 128), axis=0))
            return tuple(out)

        return one

    sums = tuple(jnp.zeros((8, 128), jnp.float32) for _ in tiles)
    for side in range(2):
        sums = lax.fori_loop(0, rows // step, sweep(side), sums)
    sums = [jnp.sum(total, axis=0, keepdims=True) for total in sums]
    least = jnp.min(functools.reduce(jnp.minimum, sums))
    for g, group in enumerate(groups):
        for k, of in enumerate(group):
            n = (g * len(group) + k) * (columns // 128 // len(group))
            some = sums[n : n + columns // 128 // len(group)]
            column_ref[pl.ds(column_of(of), 1), :] = jnp.log2(jnp.concatenate(some, axis=1))

    @pl.when(jnp.logical_not(least > 2.0**-80))
    def _():
        safe_columns(groups, score_refs, add_refs, column_ref)


def safe_columns(groups, score_refs, add_refs, column_ref):
    rows = add_refs[0].shape[0]
    step = 64
    for g, of in enumerate(groups):
        piece = score_refs[0][g].shape[1] // 2
        for k in range(2):
            at = [slice(c, c + 128) for c in range(k * piece, (k + 1) * piece, 128)]
            tops = [None] * len(at)
            for side in range(2):
                for r in range(0, rows, step):
                    add = add_refs[side][r : r + step, :]
                    for n, c in enumerate(at):
                        v = score_refs[side][g][r : r + step, c] + add
                        v = jnp.max(v.reshape(step // 8, 8, 128), axis=0)
                        tops[n] = v if tops[n] is None else jnp.maximum(tops[n], v)
            tops = [jnp.max(top, axis=0, keepdims=True) for top in tops]
            totals = [None] * len(at)
            for side in range(2):
                for r in range(0, rows, step):
                    add = add_refs[side][r : r + step, :]
                    for n, c in enumerate(at):
                        v = jnp.exp2(score_refs[side][g][r : r + step, c] + add - tops[n])
                        v = jnp.sum(v.reshape(step // 8, 8, 128), axis=0)
                        totals[n] = v if totals[n] is None else totals[n] + v
            outs = [top + jnp.log2(jnp.sum(total, axis=0, keepdims=True)) for top, total in zip(tops, totals, strict=True)]
            column_ref[pl.ds(column_of(of[k]), 1), :] = jnp.concatenate(outs, axis=1)


def map_kernel(groups, block, log_sources, *refs):
    count = len(groups)
    score_refs, refs = refs[:count], refs[count:]
    low_refs, refs = refs[:count], refs[count:]
    add_ref, parts_ref, refs = refs[0], refs[1], refs[2:]
    if log_sources is not None:
        pot_ref, out_ref, own_ref, level_ref, sum_ref = refs
    else:
        out_ref, level_ref, sum_ref = refs
    parts = [parts_ref[k] for k in range(parts_ref.shape[0])]
    level_ref[...] = log_sum(parts)
    if log_sources is not None:
        own = level_ref[pl.ds(column_of((0, False)), 1), :]
        own_ref[...] = potential_of(pot_ref, (0, False), own.shape[1]) - epsilon * (own / LOG2E - log_sources)
    rows = add_ref.shape[0]
    for g, group in enumerate(groups):
        level = jnp.concatenate([level_ref[pl.ds(column_of(of), 1), :] for of in group], axis=1)
        columns = level.shape[1]
        for start in range(0, rows, block):
            at = slice(start, start + block)
            add = add_ref[at, :]
            total = None
            weights = []
            for c in range(0, columns, 128):
                w = jnp.exp2(score_refs[g][at, c : c + 128] + add - level[:, c : c + 128])
                total = w if total is None else total + w
                weights.append(w.astype(jnp.bfloat16))
            part = jnp.dot(
                jnp.concatenate(weights, axis=1), low_refs[g][...], preferred_element_type=jnp.float32
            )
            for r in range(0, block, 128):
                k = (start + r) // 128
                if g == 0:
                    out_ref[k, 0:128, :] = part[r : r + 128, :]
                else:
                    out_ref[k, 0:128, :] += part[r : r + 128, :]
            if g == 0:
                sum_ref[at, :] = total
            else:
                sum_ref[at, :] += total
    for k in range(rows // 128):
        total = jnp.sum(sum_ref[k * 128 : (k + 1) * 128, :].T, axis=0, keepdims=True)
        out_ref[k, 128:136, :] = jnp.broadcast_to(
            jnp.concatenate([total] * (out_ref.shape[2] // 128), axis=1), (8, out_ref.shape[2])
        )


def quotient_kernel(parts_ref, out_ref):
    rows, width = out_ref.shape
    numerator = parts_ref[0, 0:rows, :]
    denominator = parts_ref[0, rows : rows + 8, 0:128]
    for k in range(1, parts_ref.shape[0]):
        numerator = numerator + parts_ref[k, 0:rows, :]
        denominator = denominator + parts_ref[k, rows : rows + 8, 0:128]
    inverse = jnp.broadcast_to(1.0 / denominator[0:1, :], (128, 128)).T
    for c in range(0, width, 128):
        out_ref[:, c : c + 128] = numerator[:, c : c + 128] * inverse


def call(kernel, name, outs, *args, scratch=(), aliases=None):
    return pl.pallas_call(
        kernel,
        out_shape=outs,
        in_specs=[spec()] * len(args),
        out_specs=[spec()] * len(outs),
        scratch_shapes=list(scratch),
        input_output_aliases=aliases or {},
        compiler_params=params(),
        name=name,
    )(*args)


def shards(source_points, target_points, target_potential):
    sizes = {name: lax.axis_size(name) for name in ("x", "zl", "c", "y", "zh")}
    across_x = sizes["x"]
    rows, width = source_points.shape
    piece = target_points.shape[0]
    tgts = sizes["y"] * sizes["zh"]
    sources = sizes["x"] * sizes["zl"] * sizes["c"]
    log_targets = math.log2(target_potential.shape[0] * tgts)
    f32, bf16 = jnp.float32, jnp.bfloat16
    share = rows // tgts

    trade = []
    for zl in range(2):
        for c in range(2):
            for zh in range(2):
                trade.append((zl * 4 + c * 2 + zh, (1 - zl) * 4 + c * 2 + (zh ^ c)))

    def traded(value):
        return lax.ppermute(value, ("zl", "c", "zh"), trade)

    def along(value, by):
        return lax.ppermute(value, "x", [(i, (i + by) % across_x) for i in range(across_x)])

    def twin(value):
        return lax.ppermute(value, "c", [(0, 1), (1, 0)])

    def along_ring(by):
        return along(target_points, by)

    other_points = twin(source_points)
    other_pot = traded(target_potential)
    blocks = {(0, False): target_points, (0, True): traded(target_points)}
    for by in (1, 2, 3):
        blocks[(across_x - by, False)] = along_ring(by)
    groups = [
        [(0, False), (0, True)],
        [(1, False), (3, False)],
        [(2, False), (1, True)],
        [(3, True), (2, True)],
    ]
    scale = 2.0 * LOG2E / (epsilon * width)
    left, squares = call(
        functools.partial(split_kernel, scale, True),
        "split",
        [VMEM((rows, 3 * width), bf16), VMEM((1, share), f32)],
        source_points,
    )
    (other_left,) = call(
        functools.partial(split_kernel, scale, False), "split", [VMEM((rows, 3 * width), bf16)], other_points
    )
    pot, other_pot = target_potential.reshape(-1, 128), other_pot.reshape(-1, 128)
    own_scores, other_scores, lows, state = [], [], [], ()
    for g, group in enumerate(groups):
        first, last = g == 0, g == len(groups) - 1
        outs = [VMEM((rows, 2 * piece), f32)] * 2 + [VMEM((2 * piece, width), bf16)] + [VMEM((rows, 128), f32)] * 4
        if last:
            outs.append(VMEM((2, rows // 128, 128), f32))
        result = call(
            functools.partial(score_kernel, group, first, last),
            "score",
            outs,
            left,
            other_left,
            *(blocks[of] for of in group),
            pot,
            other_pot,
            *state,
            scratch=[VMEM((3 * width, 2 * piece), bf16), VMEM((8, 2 * piece), f32)],
            aliases={} if first else {6 + k: 3 + k for k in range(4)},
        )
        own_scores.append(result[0])
        other_scores.append(result[1])
        lows.append(result[2])
        state = tuple(result[3:7])
        if g == 0:
            blocks[(3, False)], blocks[(1, False)], *state = lax.optimization_barrier(
                (blocks[(3, False)], blocks[(1, False)]) + state
            )
            blocks[(1, True)] = traded(blocks[(1, False)])
            blocks[(3, True)] = traded(blocks[(3, False)])
            blocks[(2, True)] = traded(blocks[(2, False)])
        if g == 1:
            pass
    levels = result[7]
    row_axes = ("c", "y", "zh")
    spread = jnp.broadcast_to(levels[None], (2 * tgts,) + levels.shape)
    row_levels = lax.all_to_all(spread, row_axes, 0, 0)
    column_level, own_source, add, other_add = call(
        functools.partial(column_kernel, groups, log_targets, width),
        "columns",
        [VMEM((2 * across_x, piece), f32), VMEM((1, share), f32), VMEM((rows, 128), f32), VMEM((rows, 128), f32)],
        *own_scores,
        *other_scores,
        row_levels,
        squares,
    )
    spread = jnp.broadcast_to(column_level[None], (2 * across_x,) + column_level.shape)
    members = []
    for layer in range(2):
        for c in range(2):
            members.append([((k * 2 + zl) * 2 + c) * 2 + (layer ^ (zl & c)) for k in range(across_x) for zl in range(2)])
    column_levels = lax.all_to_all(spread, ("x", "zl", "c", "zh"), 0, 0, axis_index_groups=members)
    scratch = [VMEM(column_level.shape, f32), VMEM((rows, 128), f32)]
    partial_out = VMEM((tgts, share + 8, width), f32)
    (other_map,) = call(
        functools.partial(map_kernel, groups, 256, None),
        "map_other",
        [partial_out],
        *other_scores,
        *lows,
        other_add,
        column_levels,
        scratch=scratch,
    )
    returned = twin(other_map)
    own_map, own_target = call(
        functools.partial(map_kernel, groups, 256, math.log(rows * sources)),
        "map",
        [partial_out, VMEM((1, piece), f32)],
        *own_scores,
        *lows,
        add,
        column_levels,
        pot,
        scratch=scratch,
    )
    summed, own_source, own_target = lax.optimization_barrier(
        (own_map + returned, own_source.reshape(share), own_target.reshape(piece))
    )
    received = lax.all_to_all(summed, ("y", "zh"), 0, 0)
    transport_map = pl.pallas_call(
        quotient_kernel,
        out_shape=jax.ShapeDtypeStruct((share, width), f32),
        in_specs=[spec()],
        out_specs=spec(),
        compiler_params=params(),
        name="quotient",
    )(received)
    return own_source, own_target, transport_map


def solution(mesh):
    fine = Mesh(mesh.devices.reshape(4, 2, 2, 4, 2), ("x", "zl", "c", "y", "zh"))
    src, tgt = ("x", "zl", "c"), ("y", "zh")
    return jax.shard_map(
        shards,
        mesh=fine,
        in_specs=(P(src, None), P(tgt + src, None), P(tgt)),
        out_specs=(P(src + tgt), P(tgt + src), P(src + tgt, None)),
        check_vma=False,
    )
```

time: 593 us -> 93.7 us (0.16)
  matrix products: 190 us -> 0 us
  blocking collectives: 190 us -> 27.5 us
  other arithmetic: 79.1 us -> 1.17 us
  waiting for transfers between devices: 85 us -> 26.3 us
  local copies, waits for them, and re-layouts: 25.9 us -> 2.33 us
  Pallas kernels: 0 us -> 21.9 us
  between operations: 14.8 us -> 0.76 us
  starting transfers between devices: 0.08 us -> 13.3 us
    dot_general x80 -> x0, matrix products: 190 us -> none  [the longest x64 167 us: pair_cost(): lax.dot_general(points, segment, (((1,), (1,)), ((), ())), precision=prec...]
    pmax x3 -> x0, blocking collectives: 99.3 us -> none  [the longest x1 52.9 us: shards(): column_high = lax.pmax(column_top, 'src')]
    reduce_sum x97 -> x0, other arithmetic: 77 us -> none  [the longest x64 67.9 us: pair_cost(): segment_squares = jnp.sum(segment * segment, axis=1)]
    psum x2 -> x0, blocking collectives: 71.9 us -> none  [the longest x1 52.9 us: shards(): lax.psum(column_total * jnp.exp(column_top - column_high), 'src')]
    reduce_scatter x1 -> x0, waiting for transfers between devices: 44.1 us -> none  [shards(): lax.psum_scatter(numerator, 'tgt', scatter_dimension=0, tiled=True)]
    all_gather x1 -> x0, waiting for transfers between devices: 40.3 us -> none  [shards(): gathered = lax.all_gather(target_points, 'src', axis=0, tiled=True)]
    all_to_all x0 -> x2, blocking collectives: none -> 27.5 us  [the longest x1 16.1 us: shards(): row_levels = lax.all_to_all(spread, row_axes, 0, 0)]
    pallas_call x0 -> x10, Pallas kernels: none -> 21.9 us  [the longest x9 21.1 us: call(): pl.pallas_call(kernel, out_shape=outs, in_specs=[spec()] * len(args), out...]
  transfers between devices with their start and end apart: 2 -> 11, of which waited for: 2 -> 5; matrix products, arithmetic and copies ran while one was open for 1% -> 1% of each run, Pallas kernels for 0% -> 10%
where the time goes in v2:
time: 93.7 us; the launch traced here: 93.2 us
  blocking collectives  27.5 us (29%)
  waiting for transfers between devices  26.3 us (28%)
  Pallas kernels  21.9 us (23%)
  starting transfers between devices  13.3 us (14%)
  local copies, waits for them, and re-layouts  2.33 us (2%)
  other arithmetic  1.17 us (1%)
    pallas_call x9, Pallas kernels, call(): pl.pallas_call(kernel, out_shape=outs, in_specs=[spec()] * len(args), out...  21.1 us
    all_to_all x1, waiting for transfers between devices, shards(): received = lax.all_to_all(summed, ('y', 'zh'), 0, 0)  17 us
    all_to_all x1, blocking collectives, shards(): row_levels = lax.all_to_all(spread, row_axes, 0, 0)  16.1 us
    all_to_all x1, blocking collectives, shards(): lax.all_to_all(spread, ('x', 'zl', 'c', 'zh'), 0, 0, axis_index_groups=me...  11.3 us
    ppermute x3, starting transfers between devices, along(): lax.ppermute(value, 'x', [(i, (i + by) % across_x) for i in range(across_...  5.05 us
    ppermute x5, starting transfers between devices, traded(): return lax.ppermute(value, ('zl', 'c', 'zh'), trade)  4.55 us
    ppermute x3, waiting for transfers between devices, along(): lax.ppermute(value, 'x', [(i, (i + by) % across_x) for i in range(across_...  4.39 us
    ppermute x5, waiting for transfers between devices, traded(): return lax.ppermute(value, ('zl', 'c', 'zh'), trade)  4.15 us
  transfers between devices with their start and end apart: 11, of which 5 were waited for; matrix products, arithmetic and copies ran while one was open for 1% of the time, Pallas kernels for 10%

profile of v2, /device:TPU:0, one launch (start us, length us, event | category | flops | bytes accessed | tf_op | source)
XLA Modules:
  0.0 93.2 jit_solution(1054393446169437947)
XLA Ops:
  0.7 2.1 %collective-permute-start.1 = (f32[256,256]{1,0:T(8,128)}, f32[256,256]{1,0:T(8,128)S(1)}, u32[]{:S(2)}, u32[]{:S(2)}) collective-permute-start(f32[256,256]{1,0:T(8,128)} %refs_2_.1), channel_id=1, source_target_pairs={{0,16},{1,17},{8,25},{9,24},{16,0},{17,1},{24,9},{25,8},{2,18},{3,... | collective-permute-start | bytes 786440 | tf_op jit(solution)/shard_map/ppermute | solution.py:292
  2.8 1.5 %collective-permute-start.3 = (f32[256,256]{1,0:T(8,128)}, f32[256,256]{1,0:T(8,128)S(1)}, u32[]{:S(2)}, u32[]{:S(2)}) collective-permute-start(f32[256,256]{1,0:T(8,128)} %refs_2_.1), channel_id=1, source_target_pairs={{0,32},{32,64},{64,96},{96,0},{1,33},{33,65},{65,97},{97,1},{2,34}... | collective-permute-start | bytes 786440 | tf_op jit(solution)/shard_map/ppermute | solution.py:295
  4.3 1.7 %collective-permute-start.4 = (f32[256,256]{1,0:T(8,128)}, f32[256,256]{1,0:T(8,128)S(1)}, u32[]{:S(2)}, u32[]{:S(2)}) collective-permute-start(f32[256,256]{1,0:T(8,128)} %refs_2_.1), channel_id=1, source_target_pairs={{0,96},{32,0},{64,32},{96,64},{1,97},{33,1},{65,33},{97,65},{2,98}... | collective-permute-start | bytes 786440 | tf_op jit(solution)/shard_map/ppermute | solution.py:295
  6.0 1.8 %collective-permute-start.5 = (f32[256,256]{1,0:T(8,128)}, f32[256,256]{1,0:T(8,128)S(1)}, u32[]{:S(2)}, u32[]{:S(2)}) collective-permute-start(f32[256,256]{1,0:T(8,128)} %refs_2_.1), channel_id=1, source_target_pairs={{0,64},{32,96},{64,0},{96,32},{1,65},{33,97},{65,1},{97,33},{2,66}... | collective-permute-start | bytes 786440 | tf_op jit(solution)/shard_map/ppermute | solution.py:295
  8.0 1.2 %copy-done = f32[1024,256]{1,0:T(8,128)S(1)} copy-done((f32[1024,256]{1,0:T(8,128)S(1)}, f32[1024,256]{1,0:T(8,128)}, u32[]{:S(2)}) %copy-start) | copy-done | bytes 1048600
  10.0 1.8 %collective-permute-done.2 = f32[4096]{0:T(1024)S(1)} collective-permute-done((f32[4096]{0:T(1024)}, f32[4096]{0:T(1024)S(1)}, u32[]{:S(2)}, u32[]{:S(2)}) %collective-permute-start.2) | collective-permute-done | bytes 16416 | tf_op jit(solution)/shard_map/ppermute | solution.py:292
  11.8 2.1 %score.4 = (f32[1024,512]{1,0:T(8,128)S(1)}, f32[1024,512]{1,0:T(8,128)S(1)}, bf16[512,256]{1,0:T(8,128)(2,1)S(1)}, f32[1024,128]{1,0:T(8,128)S(1)}, f32[1024,12...) custom-call(bf16[1024,768]{1,0:T(8,128)(2,1)S(1)} %get-tuple-element.45.refs_0_, ...), custom_call_target="tpu_custom_call" | custom-call | tf_op jit(solution)/shard_map/score/pallas_call | solution.py:262
  14.3 4.4 %collective-permute-done.5.refs_2_ = f32[256,256]{1,0:T(8,128)S(1)} collective-permute-done((f32[256,256]{1,0:T(8,128)}, f32[256,256]{1,0:T(8,128)S(1)}, u32[]{:S(2)}, u32[]{:S(2)}) %collective-permute-start.5) | collective-permute-done | bytes 262176 | tf_op jit(solution)/shard_map/ppermute | solution.py:295
  19.1 1.6 %collective-permute-start.7 = (f32[256,256]{1,0:T(8,128)S(1)}, f32[256,256]{1,0:T(8,128)S(1)}, u32[]{:S(2)}, u32[]{:S(2)}) collective-permute-start(f32[256,256]{1,0:T(8,128)S(1)} %collective-permute-done.3.refs_3_), channel_id=1, source_target_pairs={{0,16},{1,17},{8,25},{9,24},{16,0},{17,1},{24,9},{25,8},{2,18},{3,... | collective-permute-start | bytes 786440 | tf_op jit(solution)/shard_map/ppermute | solution.py:292
  20.7 2.4 %score.5 = (f32[1024,512]{1,0:T(8,128)S(1)}, f32[1024,512]{1,0:T(8,128)S(1)}, bf16[512,256]{1,0:T(8,128)(2,1)S(1)}, f32[1024,128]{1,0:T(8,128)S(1)}, f32[1024,12...) custom-call(bf16[1024,768]{1,0:T(8,128)(2,1)S(1)} %get-tuple-element, ...), custom_call_target="tpu_custom_call", output_to_operand_aliasing={{3}: (6, {}), {4}: (7, {}), {5}: (8, {}), {6}: (9, {})} | custom-call | tf_op jit(solution)/shard_map/score/pallas_call | solution.py:262
  23.1 2.4 %score.6 = (f32[1024,512]{1,0:T(8,128)S(1)}, f32[1024,512]{1,0:T(8,128)S(1)}, bf16[512,256]{1,0:T(8,128)(2,1)S(1)}, f32[1024,128]{1,0:T(8,128)S(1)}, f32[1024,12...) custom-call(bf16[1024,768]{1,0:T(8,128)(2,1)S(1)} %get-tuple-element, ...), custom_call_target="tpu_custom_call", output_to_operand_aliasing={{3}: (6, {}), {4}: (7, {}), {5}: (8, {}), {6}: (9, {})} | custom-call | tf_op jit(solution)/shard_map/score/pallas_call | solution.py:262
  25.5 2.3 %collective-permute-done.7.refs_2_ = f32[256,256]{1,0:T(8,128)S(1)} collective-permute-done((f32[256,256]{1,0:T(8,128)S(1)}, f32[256,256]{1,0:T(8,128)S(1)}, u32[]{:S(2)}, u32[]{:S(2)}) %collective-permute-start.7) | collective-permute-done | bytes 262176 | tf_op jit(solution)/shard_map/ppermute | solution.py:292
  27.9 2.6 %score.7 = (f32[1024,512]{1,0:T(8,128)S(1)}, f32[1024,512]{1,0:T(8,128)S(1)}, bf16[512,256]{1,0:T(8,128)(2,1)S(1)}, f32[1024,128]{1,0:T(8,128)S(1)}, f32[1024,12...) custom-call(bf16[1024,768]{1,0:T(8,128)(2,1)S(1)} %get-tuple-element, ...), custom_call_target="tpu_custom_call", output_to_operand_aliasing={{3}: (6, {}), {4}: (7, {}), {5}: (8, {}), {6}: (9, {})} | custom-call | tf_op jit(solution)/shard_map/score/pallas_call | solution.py:262
  30.5 16.1 %all_to_all.15.refs_8_ = f32[16,2,8,128]{3,2,1,0:T(8,128)S(1)} all-to-all(f32[16,2,8,128]{3,2,1,0:T(8,128)S(1)} %broadcast_in_dim.4), channel_id=1, replica_groups=mesh['x'=4,'zl'=2,'c'=2,'y'=4,'zh'=2] {'c','y','zh'}, dimensions={0} | all-to-all | bytes 262144 | tf_op jit(solution)/shard_map/all_to_all | solution.py:360
  46.6 6.9 %columns.1 = (f32[8,256]{1,0:T(8,128)S(1)}, f32[1,128]{1,0:T(1,128)S(1)}, f32[1024,128]{1,0:T(8,128)S(1)}, f32[1024,128]{1,0:T(8,128)S(1)}) custom-call(f32[1024,512]{1,0:T(8,128)S(1)} %get-tuple-element.46.refs_0_, f32[1024,512]{1,0:T(8,128)S(1)} %get-tuple-element.57.refs_1_, f32[1024,512]{1,0:T(8,128)S(1)} %get-tuple-element.62.refs_2_, ...), custom_call_target="tpu_custom_call" | custom-call | tf_op jit(solution)/shard_map/columns/pallas_call | solution.py:262
  53.5 11.3 %all_to_all.16.refs_9_ = f32[8,8,256]{2,1,0:T(8,128)S(1)} all-to-all(f32[8,8,256]{2,1,0:T(8,128)S(1)} %broadcast_in_dim.5), channel_id=1, replica_groups={{0,16,32,48,64,80,96,112},{8,25,40,57,72,89,104,121},{1,17,33,49,65,81,..., dimensions={0} | all-to-all | bytes 131072 | tf_op jit(solution)/shard_map/all_to_all | solution.py:375
  64.8 2.0 %map_other.1 = f32[8,136,256]{2,1,0:T(8,128)S(1)} custom-call(f32[1024,512]{1,0:T(8,128)S(1)} %get-tuple-element.72.refs_4_.refs_0_, f32[1024,512]{1,0:T(8,128)S(1)} %get-tuple-element.73.refs_5_.refs_1_, f32[1024,512]{1,0:T(8,128)S(1)} %get-tuple-element.74.refs_6_.refs_2_, f32[1024,512]{1,0:T(8,128)S(1)} %get-tuple-element.75.refs_7_.refs_3_, ...), custom_call_target="tpu_custom_call" | custom-call | tf_op jit(solution)/shard_map/map_other/pallas_call | solution.py:262
  66.9 2.0 %map.1 = (f32[8,136,256]{2,1,0:T(8,128)S(1)}, f32[1,256]{1,0:T(1,128)S(1)}) custom-call(f32[1024,512]{1,0:T(8,128)S(1)} %get-tuple-element.46.refs_0_, f32[1024,512]{1,0:T(8,128)S(1)} %get-tuple-element.57.refs_1_, f32[1024,512]{1,0:T(8,128)S(1)} %get-tuple-element.62.refs_2_, f32[1024,512]{1,0:T(8,128)S(1)} %get-tuple-element.67.refs_3_, ...), custom_call_target="tpu_custom_call" | custom-call | tf_op jit(solution)/shard_map/map/pallas_call | solution.py:262
  68.9 0.8 collective-permute-done.9
  69.6 1.2 %add.3 = f32[8,136,256]{2,1,0:T(8,128)} add(f32[8,136,256]{2,1,0:T(8,128)S(1)} %get-tuple-element.80, f32[8,136,256]{2,1,0:T(8,128)S(1)} %collective-permute-done.9) | non-fusion elementwise | flops 278528 | bytes 3342336 | tf_op jit(solution)/shard_map/add | solution.py:401
  70.8 3.6 %all-to-all-start.2 = ((f32[8,136,256]{2,1,0:T(8,128)}), f32[8,136,256]{2,1,0:T(8,128)S(1)}, u32[]{:S(2)}, u32[]{:S(2)}) async-start(f32[8,136,256]{2,1,0:T(8,128)} %add.3), calls=%async_computation.2 | async-start | bytes 2228224 | tf_op jit(solution)/shard_map/all_to_all | solution.py:403
  74.9 0.6 copy.31
  75.4 17.0 %all-to-all-done.2.parts_ref = f32[8,136,256]{2,1,0:T(8,128)S(1)} async-done(((f32[8,136,256]{2,1,0:T(8,128)}), f32[8,136,256]{2,1,0:T(8,128)S(1)}, u32[]{:S(2)}, u32[]{:S(2)}) %all-to-all-start.2) | async-done | bytes 1114144 | tf_op jit(solution)/shard_map/all_to_all | solution.py:403
  92.5 0.8 quotient.1
  (21 shorter events, 2.4 us)
Async XLA Ops:
  0.6 7.2 %collective-permute-start = (f32[1024,256]{1,0:T(8,128)}, f32[1024,256]{1,0:T(8,128)S(1)}, u32[]{:S(2)}, u32[]{:S(2)}) collective-permute-start(f32[1024,256]{1,0:T(8,128)} %x_ref.1), channel_id=1, source_target_pairs={{0,8},{8,0},{1,9},{9,1},{2,10},{10,2},{3,11},{11,3},{4,12},{12,4},... | collective-permute-start | bytes 3145736 | tf_op jit(solution)/shard_map/ppermute | solution.py:298
  0.7 11.1 %collective-permute-start.1 = (f32[256,256]{1,0:T(8,128)}, f32[256,256]{1,0:T(8,128)S(1)}, u32[]{:S(2)}, u32[]{:S(2)}) collective-permute-start(f32[256,256]{1,0:T(8,128)} %refs_2_.1), channel_id=1, source_target_pairs={{0,16},{1,17},{8,25},{9,24},{16,0},{17,1},{24,9},{25,8},{2,18},{3,... | collective-permute-start | bytes 786440 | tf_op jit(solution)/shard_map/ppermute | solution.py:292
  2.8 11.1 %collective-permute-start.3 = (f32[256,256]{1,0:T(8,128)}, f32[256,256]{1,0:T(8,128)S(1)}, u32[]{:S(2)}, u32[]{:S(2)}) collective-permute-start(f32[256,256]{1,0:T(8,128)} %refs_2_.1), channel_id=1, source_target_pairs={{0,32},{32,64},{64,96},{96,0},{1,33},{33,65},{65,97},{97,1},{2,34}... | collective-permute-start | bytes 786440 | tf_op jit(solution)/shard_map/ppermute | solution.py:295
  4.3 9.7 %collective-permute-start.4 = (f32[256,256]{1,0:T(8,128)}, f32[256,256]{1,0:T(8,128)S(1)}, u32[]{:S(2)}, u32[]{:S(2)}) collective-permute-start(f32[256,256]{1,0:T(8,128)} %refs_2_.1), channel_id=1, source_target_pairs={{0,96},{32,0},{64,32},{96,64},{1,97},{33,1},{65,33},{97,65},{2,98}... | collective-permute-start | bytes 786440 | tf_op jit(solution)/shard_map/ppermute | solution.py:295
  6.0 12.6 %collective-permute-start.5 = (f32[256,256]{1,0:T(8,128)}, f32[256,256]{1,0:T(8,128)S(1)}, u32[]{:S(2)}, u32[]{:S(2)}) collective-permute-start(f32[256,256]{1,0:T(8,128)} %refs_2_.1), channel_id=1, source_target_pairs={{0,64},{32,96},{64,0},{96,32},{1,65},{33,97},{65,1},{97,33},{2,66}... | collective-permute-start | bytes 786440 | tf_op jit(solution)/shard_map/ppermute | solution.py:295
  7.9 4.0 %collective-permute-start.2 = (f32[4096]{0:T(1024)}, f32[4096]{0:T(1024)S(1)}, u32[]{:S(2)}, u32[]{:S(2)}) collective-permute-start(f32[4096]{0:T(1024)} %param.5), channel_id=1, source_target_pairs={{0,16},{1,17},{8,25},{9,24},{16,0},{17,1},{24,9},{25,8},{2,18},{3,... | collective-permute-start | bytes 49160 | tf_op jit(solution)/shard_map/ppermute | solution.py:292
  8.0 1.2 %copy-start = (f32[1024,256]{1,0:T(8,128)S(1)}, f32[1024,256]{1,0:T(8,128)}, u32[]{:S(2)}) copy-start(f32[1024,256]{1,0:T(8,128)} %x_ref.1) | copy-start | bytes 3145732
  9.2 2.6 %copy-start.1 = (f32[4096]{0:T(1024)S(1)}, f32[4096]{0:T(1024)}, u32[]{:S(2)}) copy-start(f32[4096]{0:T(1024)} %param.5) | copy-start | bytes 49156
  9.2 2.6 %copy-start.2 = (f32[256,256]{1,0:T(8,128)S(1)}, f32[256,256]{1,0:T(8,128)}, u32[]{:S(2)}) copy-start(f32[256,256]{1,0:T(8,128)} %refs_2_.1) | copy-start | bytes 786436
  14.0 9.1 %collective-permute-start.6 = (f32[256,256]{1,0:T(8,128)S(1)}, f32[256,256]{1,0:T(8,128)S(1)}, u32[]{:S(2)}, u32[]{:S(2)}) collective-permute-start(f32[256,256]{1,0:T(8,128)S(1)} %collective-permute-done.4.refs_2_), channel_id=1, source_target_pairs={{0,16},{1,17},{8,25},{9,24},{16,0},{17,1},{24,9},{25,8},{2,18},{3,... | collective-permute-start | bytes 786440 | tf_op jit(solution)/shard_map/ppermute | solution.py:292
  18.7 6.8 %collective-permute-start.8 = (f32[256,256]{1,0:T(8,128)S(1)}, f32[256,256]{1,0:T(8,128)S(1)}, u32[]{:S(2)}, u32[]{:S(2)}) collective-permute-start(f32[256,256]{1,0:T(8,128)S(1)} %collective-permute-done.5.refs_2_), channel_id=1, source_target_pairs={{0,16},{1,17},{8,25},{9,24},{16,0},{17,1},{24,9},{25,8},{2,18},{3,... | collective-permute-start | bytes 786440 | tf_op jit(solution)/shard_map/ppermute | solution.py:292
  19.1 8.7 %collective-permute-start.7 = (f32[256,256]{1,0:T(8,128)S(1)}, f32[256,256]{1,0:T(8,128)S(1)}, u32[]{:S(2)}, u32[]{:S(2)}) collective-permute-start(f32[256,256]{1,0:T(8,128)S(1)} %collective-permute-done.3.refs_3_), channel_id=1, source_target_pairs={{0,16},{1,17},{8,25},{9,24},{16,0},{17,1},{24,9},{25,8},{2,18},{3,... | collective-permute-start | bytes 786440 | tf_op jit(solution)/shard_map/ppermute | solution.py:292
  66.8 2.8 %collective-permute-start.9 = (f32[8,136,256]{2,1,0:T(8,128)S(1)}, f32[8,136,256]{2,1,0:T(8,128)S(1)}, u32[]{:S(2)}, u32[]{:S(2)}) collective-permute-start(f32[8,136,256]{2,1,0:T(8,128)S(1)} %map_other.1), channel_id=1, source_target_pairs={{0,8},{8,0},{1,9},{9,1},{2,10},{10,2},{3,11},{11,3},{4,12},{12,4},... | collective-permute-start | bytes 3342344 | tf_op jit(solution)/shard_map/ppermute | solution.py:298
  70.8 21.7 %all-to-all-start.2 = ((f32[8,136,256]{2,1,0:T(8,128)}), f32[8,136,256]{2,1,0:T(8,128)S(1)}, u32[]{:S(2)}, u32[]{:S(2)}) async-start(f32[8,136,256]{2,1,0:T(8,128)} %add.3), calls=%async_computation.2 | async-start | bytes 2228224 | tf_op jit(solution)/shard_map/all_to_all | solution.py:403

commit v3 on v2

--- a/solution.py
+++ b/solution.py
@@ -55,10 +55,19 @@
     return place(of) * 2 + half_of(of)
 
 
-def potential_of(pot_ref, of, piece):
+def potential_of(pot_ref, base, of, piece):
     lines = piece // 128
-    start = piece_of(of) * lines
-    return jnp.concatenate([pot_ref[pl.ds(start + k, 1), :] for k in range(lines)], axis=1)
+    start = base + piece_of(of) * lines
+    return jnp.concatenate([pot_ref[pl.ds(start + k, 1), :][:, 0:128] for k in range(lines)], axis=1)
+
+
+def pack_kernel(starts, *refs):
+    out_ref = refs[-1]
+    for start, ref in zip(starts, refs[-1 - len(starts) : -1], strict=True):
+        rows, width = ref.shape
+        out_ref[start : start + rows, 0:width] = ref[...]
+        if width < out_ref.shape[1]:
+            out_ref[start : start + rows, width:] = jnp.zeros((rows, out_ref.shape[1] - width), jnp.float32)
 
 
 def score_rows(x_ref, right_ref, offset_ref, old, score_ref, top_ref, total_ref, block):
@@ -80,18 +89,19 @@
         total_ref[at, :] = total
 
 
-def score_kernel(group, first, last, *refs):
-    left_refs, t_refs, pot_refs, refs = refs[:2], refs[2:4], refs[4:6], refs[6:]
+def score_kernel(group, piece, sources, base, first, last, *refs):
+    left_refs, refs = refs[:2], refs[2:]
+    block_refs, pot_ref, refs = refs[: len(sources)], refs[len(sources)], refs[len(sources) + 1 :]
     old = (None, None)
     if not first:
         old, refs = (refs[0:2], refs[2:4]), refs[4:]
     score_refs, low_ref, state_refs, refs = refs[:2], refs[2], (refs[3:5], refs[5:7]), refs[7:]
     right_ref, offset_ref = refs[-2:]
-    piece, width = t_refs[0].shape
+    width = low_ref.shape[1]
     factor = LOG2E / epsilon
     for k, of in enumerate(group):
         at = slice(k * piece, (k + 1) * piece)
-        t = t_refs[k][...]
+        t = block_refs[k][sources[k] : sources[k] + piece, :]
         low_ref[at, :] = t.astype(jnp.bfloat16)
         tt = t.T
         high = tt.astype(jnp.bfloat16)
@@ -100,7 +110,7 @@
         right_ref[width : 2 * width, at] = low
         right_ref[2 * width : 3 * width, at] = high
         squares = jnp.sum(tt * tt, axis=0, keepdims=True)
-        potential = potential_of(pot_refs[int(of[1])], of, piece)
+        potential = potential_of(pot_ref, base, of, piece)
         offset_ref[0:1, at] = potential * factor - squares * (factor / width)
     for side in range(2):
         score_rows(left_refs[side], right_ref, offset_ref, old[side], score_refs[side], *state_refs[side], 256)
@@ -212,7 +222,7 @@
     level_ref[...] = log_sum(parts)
     if log_sources is not None:
         own = level_ref[pl.ds(column_of((0, False)), 1), :]
-        own_ref[...] = potential_of(pot_ref, (0, False), own.shape[1]) - epsilon * (own / LOG2E - log_sources)
+        own_ref[...] = potential_of(pot_ref, 0, (0, False), own.shape[1]) - epsilon * (own / LOG2E - log_sources)
     rows = add_ref.shape[0]
     for g, group in enumerate(groups):
         level = jnp.concatenate([level_ref[pl.ds(column_of(of), 1), :] for of in group], axis=1)
@@ -246,7 +256,9 @@
         )
 
 
-def quotient_kernel(parts_ref, out_ref):
+def quotient_kernel(parts_ref, source_ref, target_ref, own_source_ref, own_target_ref, out_ref):
+    own_source_ref[...] = source_ref[0, :]
+    own_target_ref[...] = target_ref[0, :]
     rows, width = out_ref.shape
     numerator = parts_ref[0, 0:rows, :]
     denominator = parts_ref[0, rows : rows + 8, 0:128]
@@ -297,31 +309,37 @@
     def twin(value):
         return lax.ppermute(value, "c", [(0, 1), (1, 0)])
 
-    def along_ring(by):
-        return along(target_points, by)
-
     other_points = twin(source_points)
-    other_pot = traded(target_potential)
-    blocks = {(0, False): target_points, (0, True): traded(target_points)}
-    for by in (1, 2, 3):
-        blocks[(across_x - by, False)] = along_ring(by)
+    pot = target_potential.reshape(-1, 128)
+    behind = along(target_points, 1)
+    ahead = along(target_points, across_x - 1)
+    far = along(target_points, 2)
+    parcel = [VMEM((2 * piece + pot.shape[0], width), f32)]
+    (parcel_start,) = call(functools.partial(pack_kernel, (0, 2 * piece)), "pack", parcel, target_points, pot)
+    points = source_points
+    (near,) = call(
+        functools.partial(pack_kernel, (piece,)), "pack", parcel, parcel_start, behind, aliases={0: 0}
+    )
+    near = traded(near)
     groups = [
-        [(0, False), (0, True)],
-        [(1, False), (3, False)],
-        [(2, False), (1, True)],
-        [(3, True), (2, True)],
+        [(0, False), (3, False)],
+        [(1, False), (2, False)],
+        [(0, True), (3, True)],
+        [(1, True), (2, True)],
     ]
+    blocks = [[target_points, behind], [ahead, far], [near, near], None]
+    starts = [(0, 0), (0, 0), (0, piece), (0, piece)]
+    pots = [(pot, 0), (pot, 0), (near, 2 * piece), (near, 2 * piece)]
     scale = 2.0 * LOG2E / (epsilon * width)
     left, squares = call(
         functools.partial(split_kernel, scale, True),
         "split",
         [VMEM((rows, 3 * width), bf16), VMEM((1, share), f32)],
-        source_points,
+        points,
     )
     (other_left,) = call(
         functools.partial(split_kernel, scale, False), "split", [VMEM((rows, 3 * width), bf16)], other_points
     )
-    pot, other_pot = target_potential.reshape(-1, 128), other_pot.reshape(-1, 128)
     own_scores, other_scores, lows, state = [], [], [], ()
     for g, group in enumerate(groups):
         first, last = g == 0, g == len(groups) - 1
@@ -329,31 +347,29 @@
         if last:
             outs.append(VMEM((2, rows // 128, 128), f32))
         result = call(
-            functools.partial(score_kernel, group, first, last),
+            functools.partial(score_kernel, group, piece, starts[g], pots[g][1], first, last),
             "score",
             outs,
             left,
             other_left,
-            *(blocks[of] for of in group),
-            pot,
-            other_pot,
+            *blocks[g],
+            pots[g][0],
             *state,
             scratch=[VMEM((3 * width, 2 * piece), bf16), VMEM((8, 2 * piece), f32)],
-            aliases={} if first else {6 + k: 3 + k for k in range(4)},
+            aliases={} if first else {3 + len(blocks[g]) + k: 3 + k for k in range(4)},
         )
         own_scores.append(result[0])
         other_scores.append(result[1])
         lows.append(result[2])
         state = tuple(result[3:7])
         if g == 0:
-            blocks[(3, False)], blocks[(1, False)], *state = lax.optimization_barrier(
-                (blocks[(3, False)], blocks[(1, False)]) + state
+            ahead, far, *state = lax.optimization_barrier((ahead, far) + state)
+            blocks[1] = [ahead, far]
+            (rest,) = call(
+                functools.partial(pack_kernel, (0, piece)), "pack", [VMEM((2 * piece, width), f32)], ahead, far
             )
-            blocks[(1, True)] = traded(blocks[(1, False)])
-            blocks[(3, True)] = traded(blocks[(3, False)])
-            blocks[(2, True)] = traded(blocks[(2, False)])
-        if g == 1:
-            pass
+            rest = traded(rest)
+            blocks[3] = [rest, rest]
     levels = result[7]
     row_axes = ("c", "y", "zh")
     spread = jnp.broadcast_to(levels[None], (2 * tgts,) + levels.shape)
@@ -397,19 +413,10 @@
         pot,
         scratch=scratch,
     )
-    summed, own_source, own_target = lax.optimization_barrier(
-        (own_map + returned, own_source.reshape(share), own_target.reshape(piece))
-    )
+    summed = own_map + returned
     received = lax.all_to_all(summed, ("y", "zh"), 0, 0)
-    transport_map = pl.pallas_call(
-        quotient_kernel,
-        out_shape=jax.ShapeDtypeStruct((share, width), f32),
-        in_specs=[spec()],
-        out_specs=spec(),
-        compiler_params=params(),
-        name="quotient",
-    )(received)
-    return own_source, own_target, transport_map
+    results = [jax.ShapeDtypeStruct(dims, f32) for dims in ((share,), (piece,), (share, width))]
+    return tuple(call(quotient_kernel, "quotient", results, received, own_source, own_target))
 
 
 def solution(mesh):

time: 93.7 us -> 89.4 us (0.954)
  blocking collectives: 27.5 us -> 47 us
  waiting for transfers between devices: 26.3 us -> 8.06 us
  starting transfers between devices: 13.3 us -> 9.45 us
  other arithmetic: 1.17 us -> 0.14 us
    all_to_all x0 -> x1, blocking collectives: none -> 21.2 us  [shards(): received = lax.all_to_all(summed, ('y', 'zh'), 0, 0)]
    all_to_all x1 -> x0, waiting for transfers between devices: 17 us -> none  [shards(): received = lax.all_to_all(summed, ('y', 'zh'), 0, 0)]
    all_to_all x1 -> x0, starting transfers between devices: 3.56 us -> none  [shards(): received = lax.all_to_all(summed, ('y', 'zh'), 0, 0)]
    ppermute x5 -> x2, waiting for transfers between devices: 4.15 us -> 2.49 us  [traded(): return lax.ppermute(value, ('zl', 'c', 'zh'), trade)]
    all_to_all x1, blocking collectives: 11.3 us -> 9.77 us  [shards(): lax.all_to_all(spread, ('x', 'zl', 'c', 'zh'), 0, 0, axis_index_groups=me...]
    add x1, other arithmetic: 1.17 us -> 0.14 us  [shards(): summed = own_map + returned]
    pallas_call x9 -> x13, Pallas kernels: 21.1 us -> 21.9 us  [call(): pl.pallas_call(kernel, out_shape=outs, in_specs=[spec()] * len(args), out...]
    unnamed x8 -> x10, local copies, waits for them, and re-layouts: 2.31 us -> 1.72 us
  transfers between devices with their start and end apart: 11 -> 7, of which waited for: 5 -> 4; matrix products, arithmetic and copies ran while one was open for 1% -> 0% of each run, Pallas kernels for 10% -> 11%
where the time goes in v3:
time: 89.4 us; the launch traced here: 89.1 us
  blocking collectives  47 us (53%)
  Pallas kernels  21.9 us (24%)
  starting transfers between devices  9.45 us (11%)
  waiting for transfers between devices  8.06 us (9%)
  local copies, waits for them, and re-layouts  1.74 us (2%)
    pallas_call x13, Pallas kernels, call(): pl.pallas_call(kernel, out_shape=outs, in_specs=[spec()] * len(args), out...  21.9 us
    all_to_all x1, blocking collectives, shards(): received = lax.all_to_all(summed, ('y', 'zh'), 0, 0)  21.2 us
    all_to_all x1, blocking collectives, shards(): row_levels = lax.all_to_all(spread, row_axes, 0, 0)  16 us
    all_to_all x1, blocking collectives, shards(): lax.all_to_all(spread, ('x', 'zl', 'c', 'zh'), 0, 0, axis_index_groups=me...  9.77 us
    ppermute x3, starting transfers between devices, along(): lax.ppermute(value, 'x', [(i, (i + by) % across_x) for i in range(across_...  5.2 us
    ppermute x3, waiting for transfers between devices, along(): lax.ppermute(value, 'x', [(i, (i + by) % across_x) for i in range(across_...  4.82 us
    ppermute x2, starting transfers between devices, traded(): return lax.ppermute(value, ('zl', 'c', 'zh'), trade)  4.08 us
    ppermute x2, waiting for transfers between devices, traded(): return lax.ppermute(value, ('zl', 'c', 'zh'), trade)  2.49 us
  transfers between devices with their start and end apart: 7, of which 4 were waited for; matrix products, arithmetic and copies ran while one was open for 0% of the time, Pallas kernels for 11%

profile of v3, /device:TPU:0, one launch (start us, length us, event | category | flops | bytes accessed | tf_op | source)
XLA Modules:
  0.0 89.1 jit_solution(17482190094166422201)
XLA Ops:
  0.7 1.6 %collective-permute-start.1 = (f32[256,256]{1,0:T(8,128)}, f32[256,256]{1,0:T(8,128)S(1)}, u32[]{:S(2)}, u32[]{:S(2)}) collective-permute-start(f32[256,256]{1,0:T(8,128)} %refs_0_.1), channel_id=1, source_target_pairs={{0,32},{32,64},{64,96},{96,0},{1,33},{33,65},{65,97},{97,1},{2,34}... | collective-permute-start | bytes 786440 | tf_op jit(solution)/shard_map/ppermute | solution.py:307
  2.4 1.7 %collective-permute-start.2 = (f32[256,256]{1,0:T(8,128)}, f32[256,256]{1,0:T(8,128)S(1)}, u32[]{:S(2)}, u32[]{:S(2)}) collective-permute-start(f32[256,256]{1,0:T(8,128)} %refs_0_.1), channel_id=1, source_target_pairs={{0,96},{32,0},{64,32},{96,64},{1,97},{33,1},{65,33},{97,65},{2,98}... | collective-permute-start | bytes 786440 | tf_op jit(solution)/shard_map/ppermute | solution.py:307
  4.0 1.9 %collective-permute-start.3 = (f32[256,256]{1,0:T(8,128)}, f32[256,256]{1,0:T(8,128)S(1)}, u32[]{:S(2)}, u32[]{:S(2)}) collective-permute-start(f32[256,256]{1,0:T(8,128)} %refs_0_.1), channel_id=1, source_target_pairs={{0,64},{32,96},{64,0},{96,32},{1,65},{33,97},{65,1},{97,33},{2,66}... | collective-permute-start | bytes 786440 | tf_op jit(solution)/shard_map/ppermute | solution.py:307
  5.9 1.0 %copy-done = f32[256,256]{1,0:T(8,128)S(1)} copy-done((f32[256,256]{1,0:T(8,128)S(1)}, f32[256,256]{1,0:T(8,128)}, u32[]{:S(2)}) %copy-start) | copy-done | bytes 262168
  6.9 0.7 copy-done.3
  7.7 3.2 %collective-permute-done.1.refs_3_.refs_1_ = f32[256,256]{1,0:T(8,128)S(1)} collective-permute-done((f32[256,256]{1,0:T(8,128)}, f32[256,256]{1,0:T(8,128)S(1)}, u32[]{:S(2)}, u32[]{:S(2)}) %collective-permute-start.1) | collective-permute-done | bytes 262176 | tf_op jit(solution)/shard_map/ppermute | solution.py:307
  10.9 2.1 %collective-permute-start.4 = (f32[544,256]{1,0:T(8,128)S(1)}, f32[544,256]{1,0:T(8,128)S(1)}, u32[]{:S(2)}, u32[]{:S(2)}) collective-permute-start(f32[544,256]{1,0:T(8,128)S(1)} %pack.4), channel_id=1, source_target_pairs={{0,16},{1,17},{8,25},{9,24},{16,0},{17,1},{24,9},{25,8},{2,18},{3,... | collective-permute-start | bytes 1671176 | tf_op jit(solution)/shard_map/ppermute | solution.py:304
  13.0 0.5 split.2
  13.5 0.3 split.3.refs_1_
  13.8 2.1 %score.4 = (f32[1024,512]{1,0:T(8,128)S(1)}, f32[1024,512]{1,0:T(8,128)S(1)}, bf16[512,256]{1,0:T(8,128)(2,1)S(1)}, f32[1024,128]{1,0:T(8,128)S(1)}, f32[1024,12...) custom-call(bf16[1024,768]{1,0:T(8,128)(2,1)S(1)} %get-tuple-element.42.refs_0_, ...), custom_call_target="tpu_custom_call" | custom-call | tf_op jit(solution)/shard_map/score/pallas_call | solution.py:274
  16.0 1.6 %collective-permute-done.3.refs_3_.refs_1_ = f32[256,256]{1,0:T(8,128)S(1)} collective-permute-done((f32[256,256]{1,0:T(8,128)}, f32[256,256]{1,0:T(8,128)S(1)}, u32[]{:S(2)}, u32[]{:S(2)}) %collective-permute-start.3) | collective-permute-done | bytes 262176 | tf_op jit(solution)/shard_map/ppermute | solution.py:307
  17.6 2.0 %collective-permute-start.5 = (f32[512,256]{1,0:T(8,128)S(1)}, f32[512,256]{1,0:T(8,128)S(1)}, u32[]{:S(2)}, u32[]{:S(2)}) collective-permute-start(f32[512,256]{1,0:T(8,128)S(1)} %pack.5), channel_id=1, source_target_pairs={{0,16},{1,17},{8,25},{9,24},{16,0},{17,1},{24,9},{25,8},{2,18},{3,... | collective-permute-start | bytes 1572872 | tf_op jit(solution)/shard_map/ppermute | solution.py:304
  19.6 2.4 %score.5 = (f32[1024,512]{1,0:T(8,128)S(1)}, f32[1024,512]{1,0:T(8,128)S(1)}, bf16[512,256]{1,0:T(8,128)(2,1)S(1)}, f32[1024,128]{1,0:T(8,128)S(1)}, f32[1024,12...) custom-call(bf16[1024,768]{1,0:T(8,128)(2,1)S(1)} %get-tuple-element, ...), custom_call_target="tpu_custom_call", output_to_operand_aliasing={{3}: (5, {}), {4}: (6, {}), {5}: (7, {}), {6}: (8, {})} | custom-call | tf_op jit(solution)/shard_map/score/pallas_call | solution.py:274
  22.0 2.4 %score.6 = (f32[1024,512]{1,0:T(8,128)S(1)}, f32[1024,512]{1,0:T(8,128)S(1)}, bf16[512,256]{1,0:T(8,128)(2,1)S(1)}, f32[1024,128]{1,0:T(8,128)S(1)}, f32[1024,12...) custom-call(bf16[1024,768]{1,0:T(8,128)(2,1)S(1)} %get-tuple-element, ...), custom_call_target="tpu_custom_call", output_to_operand_aliasing={{3}: (5, {}), {4}: (6, {}), {5}: (7, {}), {6}: (8, {})} | custom-call | tf_op jit(solution)/shard_map/score/pallas_call | solution.py:274
  24.4 2.5 %collective-permute-done.5.refs_2_.refs_3_ = f32[512,256]{1,0:T(8,128)S(1)} collective-permute-done((f32[512,256]{1,0:T(8,128)S(1)}, f32[512,256]{1,0:T(8,128)S(1)}, u32[]{:S(2)}, u32[]{:S(2)}) %collective-permute-start.5) | collective-permute-done | bytes 524320 | tf_op jit(solution)/shard_map/ppermute | solution.py:304
  26.9 2.6 %score.7 = (f32[1024,512]{1,0:T(8,128)S(1)}, f32[1024,512]{1,0:T(8,128)S(1)}, bf16[512,256]{1,0:T(8,128)(2,1)S(1)}, f32[1024,128]{1,0:T(8,128)S(1)}, f32[1024,12...) custom-call(bf16[1024,768]{1,0:T(8,128)(2,1)S(1)} %get-tuple-element, ...), custom_call_target="tpu_custom_call", output_to_operand_aliasing={{3}: (5, {}), {4}: (6, {}), {5}: (7, {}), {6}: (8, {})} | custom-call | tf_op jit(solution)/shard_map/score/pallas_call | solution.py:274
  29.4 16.0 %all_to_all.15.refs_8_ = f32[16,2,8,128]{3,2,1,0:T(8,128)S(1)} all-to-all(f32[16,2,8,128]{3,2,1,0:T(8,128)S(1)} %broadcast_in_dim.4), channel_id=1, replica_groups=mesh['x'=4,'zl'=2,'c'=2,'y'=4,'zh'=2] {'c','y','zh'}, dimensions={0} | all-to-all | bytes 262144 | tf_op jit(solution)/shard_map/all_to_all | solution.py:376
  45.5 6.9 %columns.1 = (f32[8,256]{1,0:T(8,128)S(1)}, f32[1,128]{1,0:T(1,128)S(1)}, f32[1024,128]{1,0:T(8,128)S(1)}, f32[1024,128]{1,0:T(8,128)S(1)}) custom-call(f32[1024,512]{1,0:T(8,128)S(1)} %get-tuple-element.43.refs_0_, f32[1024,512]{1,0:T(8,128)S(1)} %get-tuple-element.54.refs_1_, f32[1024,512]{1,0:T(8,128)S(1)} %get-tuple-element.59.refs_2_, ...), custom_call_target="tpu_custom_call" | custom-call | tf_op jit(solution)/shard_map/columns/pallas_call | solution.py:274
  52.4 9.8 %all_to_all.16.refs_9_ = f32[8,8,256]{2,1,0:T(8,128)S(1)} all-to-all(f32[8,8,256]{2,1,0:T(8,128)S(1)} %broadcast_in_dim.5), channel_id=1, replica_groups={{0,16,32,48,64,80,96,112},{8,25,40,57,72,89,104,121},{1,17,33,49,65,81,..., dimensions={0} | all-to-all | bytes 131072 | tf_op jit(solution)/shard_map/all_to_all | solution.py:391
  62.2 2.0 %map_other.1 = f32[8,136,256]{2,1,0:T(8,128)S(1)} custom-call(f32[1024,512]{1,0:T(8,128)S(1)} %get-tuple-element.69.refs_4_.refs_0_, f32[1024,512]{1,0:T(8,128)S(1)} %get-tuple-element.70.refs_5_.refs_1_, f32[1024,512]{1,0:T(8,128)S(1)} %get-tuple-element.71.refs_6_.refs_2_, f32[1024,512]{1,0:T(8,128)S(1)} %get-tuple-element.72.refs_7_.refs_3_, ...), custom_call_target="tpu_custom_call" | custom-call | tf_op jit(solution)/shard_map/map_other/pallas_call | solution.py:274
  64.2 2.0 %map.1 = (f32[8,136,256]{2,1,0:T(8,128)S(1)}, f32[1,256]{1,0:T(1,128)S(1)}) custom-call(f32[1024,512]{1,0:T(8,128)S(1)} %get-tuple-element.43.refs_0_, f32[1024,512]{1,0:T(8,128)S(1)} %get-tuple-element.54.refs_1_, f32[1024,512]{1,0:T(8,128)S(1)} %get-tuple-element.59.refs_2_, f32[1024,512]{1,0:T(8,128)S(1)} %get-tuple-element.64.refs_3_, ...), custom_call_target="tpu_custom_call" | custom-call | tf_op jit(solution)/shard_map/map/pallas_call | solution.py:274
  66.2 0.8 collective-permute-done.6
  67.1 21.2 %all_to_all.17.parts_ref = f32[8,136,256]{2,1,0:T(8,128)S(1)} all-to-all(f32[8,136,256]{2,1,0:T(8,128)S(1)} %add.3), channel_id=1, replica_groups=mesh['x'=4,'zl'=2,'c'=2,'y'=4,'zh'=2] {'y','zh'}, dimensions={0} | all-to-all | bytes 2228224 | tf_op jit(solution)/shard_map/all_to_all | solution.py:417
  88.3 0.8 quotient.1
  (19 shorter events, 0.4 us)
Async XLA Ops:
  0.6 12.9 %collective-permute-start = (f32[1024,256]{1,0:T(8,128)}, f32[1024,256]{1,0:T(8,128)S(1)}, u32[]{:S(2)}, u32[]{:S(2)}) collective-permute-start(f32[1024,256]{1,0:T(8,128)} %x_ref.1), channel_id=1, source_target_pairs={{0,8},{8,0},{1,9},{9,1},{2,10},{10,2},{3,11},{11,3},{4,12},{12,4},... | collective-permute-start | bytes 3145736 | tf_op jit(solution)/shard_map/ppermute | solution.py:310
  0.7 10.1 %collective-permute-start.1 = (f32[256,256]{1,0:T(8,128)}, f32[256,256]{1,0:T(8,128)S(1)}, u32[]{:S(2)}, u32[]{:S(2)}) collective-permute-start(f32[256,256]{1,0:T(8,128)} %refs_0_.1), channel_id=1, source_target_pairs={{0,32},{32,64},{64,96},{96,0},{1,33},{33,65},{65,97},{97,1},{2,34}... | collective-permute-start | bytes 786440 | tf_op jit(solution)/shard_map/ppermute | solution.py:307
  2.4 13.6 %collective-permute-start.2 = (f32[256,256]{1,0:T(8,128)}, f32[256,256]{1,0:T(8,128)S(1)}, u32[]{:S(2)}, u32[]{:S(2)}) collective-permute-start(f32[256,256]{1,0:T(8,128)} %refs_0_.1), channel_id=1, source_target_pairs={{0,96},{32,0},{64,32},{96,64},{1,97},{33,1},{65,33},{97,65},{2,98}... | collective-permute-start | bytes 786440 | tf_op jit(solution)/shard_map/ppermute | solution.py:307
  4.0 13.5 %collective-permute-start.3 = (f32[256,256]{1,0:T(8,128)}, f32[256,256]{1,0:T(8,128)S(1)}, u32[]{:S(2)}, u32[]{:S(2)}) collective-permute-start(f32[256,256]{1,0:T(8,128)} %refs_0_.1), channel_id=1, source_target_pairs={{0,64},{32,96},{64,0},{96,32},{1,65},{33,97},{65,1},{97,33},{2,66}... | collective-permute-start | bytes 786440 | tf_op jit(solution)/shard_map/ppermute | solution.py:307
  5.9 1.0 %copy-start = (f32[256,256]{1,0:T(8,128)S(1)}, f32[256,256]{1,0:T(8,128)}, u32[]{:S(2)}) copy-start(f32[256,256]{1,0:T(8,128)} %refs_0_.1) | copy-start | bytes 786436
  6.9 0.7 copy-start.3
  7.6 5.4 %copy-start.2 = (f32[1024,256]{1,0:T(8,128)S(1)}, f32[1024,256]{1,0:T(8,128)}, u32[]{:S(2)}) copy-start(f32[1024,256]{1,0:T(8,128)} %x_ref.1) | copy-start | bytes 3145732
  10.9 2.9 %copy-start.1 = (f32[256,256]{1,0:T(8,128)S(1)}, f32[256,256]{1,0:T(8,128)}, u32[]{:S(2)}) copy-start(f32[256,256]{1,0:T(8,128)} %refs_0_.1) | copy-start | bytes 786436
  10.9 2.9 %copy-start.4 = (f32[4096]{0:T(1024)S(1)}, f32[4096]{0:T(1024)}, u32[]{:S(2)}) copy-start(f32[4096]{0:T(1024)} %param.5) | copy-start | bytes 49156
  10.9 11.1 %collective-permute-start.4 = (f32[544,256]{1,0:T(8,128)S(1)}, f32[544,256]{1,0:T(8,128)S(1)}, u32[]{:S(2)}, u32[]{:S(2)}) collective-permute-start(f32[544,256]{1,0:T(8,128)S(1)} %pack.4), channel_id=1, source_target_pairs={{0,16},{1,17},{8,25},{9,24},{16,0},{17,1},{24,9},{25,8},{2,18},{3,... | collective-permute-start | bytes 1671176 | tf_op jit(solution)/shard_map/ppermute | solution.py:304
  17.6 9.3 %collective-permute-start.5 = (f32[512,256]{1,0:T(8,128)S(1)}, f32[512,256]{1,0:T(8,128)S(1)}, u32[]{:S(2)}, u32[]{:S(2)}) collective-permute-start(f32[512,256]{1,0:T(8,128)S(1)} %pack.5), channel_id=1, source_target_pairs={{0,16},{1,17},{8,25},{9,24},{16,0},{17,1},{24,9},{25,8},{2,18},{3,... | collective-permute-start | bytes 1572872 | tf_op jit(solution)/shard_map/ppermute | solution.py:304
  64.2 2.8 %collective-permute-start.6 = (f32[8,136,256]{2,1,0:T(8,128)S(1)}, f32[8,136,256]{2,1,0:T(8,128)S(1)}, u32[]{:S(2)}, u32[]{:S(2)}) collective-permute-start(f32[8,136,256]{2,1,0:T(8,128)S(1)} %map_other.1), channel_id=1, source_target_pairs={{0,8},{8,0},{1,9},{9,1},{2,10},{10,2},{3,11},{11,3},{4,12},{12,4},... | collective-permute-start | bytes 3342344 | tf_op jit(solution)/shard_map/ppermute | solution.py:310

commit v4 on v3

--- a/solution.py
+++ b/solution.py
@@ -215,45 +215,40 @@
     low_refs, refs = refs[:count], refs[count:]
     add_ref, parts_ref, refs = refs[0], refs[1], refs[2:]
     if log_sources is not None:
-        pot_ref, out_ref, own_ref, level_ref, sum_ref = refs
+        pot_ref, out_ref, own_ref, level_ref = refs
     else:
-        out_ref, level_ref, sum_ref = refs
+        out_ref, level_ref = refs
     parts = [parts_ref[k] for k in range(parts_ref.shape[0])]
     level_ref[...] = log_sum(parts)
     if log_sources is not None:
         own = level_ref[pl.ds(column_of((0, False)), 1), :]
         own_ref[...] = potential_of(pot_ref, 0, (0, False), own.shape[1]) - epsilon * (own / LOG2E - log_sources)
     rows = add_ref.shape[0]
-    for g, group in enumerate(groups):
-        level = jnp.concatenate([level_ref[pl.ds(column_of(of), 1), :] for of in group], axis=1)
-        columns = level.shape[1]
-        for start in range(0, rows, block):
-            at = slice(start, start + block)
-            add = add_ref[at, :]
-            total = None
+    levels = [
+        jnp.concatenate([level_ref[pl.ds(column_of(of), 1), :] for of in group], axis=1) for group in groups
+    ]
+    for start in range(0, rows, block):
+        at = slice(start, start + block)
+        add = add_ref[at, :]
+        total = None
+        result = None
+        for g, level in enumerate(levels):
             weights = []
-            for c in range(0, columns, 128):
-                w = jnp.exp2(score_refs[g][at, c : c + 128] + add - level[:, c : c + 128])
-                total = w if total is None else total + w
-                weights.append(w.astype(jnp.bfloat16))
+            for c in range(0, level.shape[1], 128):
+                w = jnp.exp2(score_refs[g][at, c : c + 128] + add - level[:, c : c + 128]).astype(jnp.bfloat16)
+                total = w.astype(jnp.float32) if total is None else total + w.astype(jnp.float32)
+                weights.append(w)
             part = jnp.dot(
                 jnp.concatenate(weights, axis=1), low_refs[g][...], preferred_element_type=jnp.float32
             )
-            for r in range(0, block, 128):
-                k = (start + r) // 128
-                if g == 0:
-                    out_ref[k, 0:128, :] = part[r : r + 128, :]
-                else:
-                    out_ref[k, 0:128, :] += part[r : r + 128, :]
-            if g == 0:
-                sum_ref[at, :] = total
-            else:
-                sum_ref[at, :] += total
-    for k in range(rows // 128):
-        total = jnp.sum(sum_ref[k * 128 : (k + 1) * 128, :].T, axis=0, keepdims=True)
-        out_ref[k, 128:136, :] = jnp.broadcast_to(
-            jnp.concatenate([total] * (out_ref.shape[2] // 128), axis=1), (8, out_ref.shape[2])
-        )
+            result = part if result is None else result + part
+        for r in range(0, block, 128):
+            k = (start + r) // 128
+            out_ref[k, 0:128, :] = result[r : r + 128, :]
+            sums = jnp.sum(total[r : r + 128, :].T, axis=0, keepdims=True)
+            out_ref[k, 128:136, :] = jnp.broadcast_to(
+                jnp.concatenate([sums] * (out_ref.shape[2] // 128), axis=1), (8, out_ref.shape[2])
+            )
 
 
 def quotient_kernel(parts_ref, source_ref, target_ref, own_source_ref, own_target_ref, out_ref):
@@ -311,9 +306,9 @@
 
     other_points = twin(source_points)
     pot = target_potential.reshape(-1, 128)
+    far = along(target_points, 2)
     behind = along(target_points, 1)
     ahead = along(target_points, across_x - 1)
-    far = along(target_points, 2)
     parcel = [VMEM((2 * piece + pot.shape[0], width), f32)]
     (parcel_start,) = call(functools.partial(pack_kernel, (0, 2 * piece)), "pack", parcel, target_points, pot)
     points = source_points
@@ -363,7 +358,7 @@
         lows.append(result[2])
         state = tuple(result[3:7])
         if g == 0:
-            ahead, far, *state = lax.optimization_barrier((ahead, far) + state)
+            ahead, far, squares = lax.optimization_barrier((ahead, far, squares))
             blocks[1] = [ahead, far]
             (rest,) = call(
                 functools.partial(pack_kernel, (0, piece)), "pack", [VMEM((2 * piece, width), f32)], ahead, far
@@ -389,10 +384,10 @@
         for c in range(2):
             members.append([((k * 2 + zl) * 2 + c) * 2 + (layer ^ (zl & c)) for k in range(across_x) for zl in range(2)])
     column_levels = lax.all_to_all(spread, ("x", "zl", "c", "zh"), 0, 0, axis_index_groups=members)
-    scratch = [VMEM(column_level.shape, f32), VMEM((rows, 128), f32)]
+    scratch = [VMEM(column_level.shape, f32)]
     partial_out = VMEM((tgts, share + 8, width), f32)
     (other_map,) = call(
-        functools.partial(map_kernel, groups, 256, None),
+        functools.partial(map_kernel, groups, 512, None),
         "map_other",
         [partial_out],
         *other_scores,
@@ -403,7 +398,7 @@
     )
     returned = twin(other_map)
     own_map, own_target = call(
-        functools.partial(map_kernel, groups, 256, math.log(rows * sources)),
+        functools.partial(map_kernel, groups, 512, math.log(rows * sources)),
         "map",
         [partial_out, VMEM((1, piece), f32)],
         *own_scores,

time: 89.4 us -> 89 us (level)
    ppermute x3, waiting for transfers between devices: 4.82 us -> 7.24 us  [along(): lax.ppermute(value, 'x', [(i, (i + by) % across_x) for i in range(across_...]
    ppermute x2, waiting for transfers between devices: 2.49 us -> 0.07 us  [traded(): return lax.ppermute(value, ('zl', 'c', 'zh'), trade)]
where the time goes in v4:
time: 89 us; the launch traced here: 88.7 us
  blocking collectives  47 us (53%)
  Pallas kernels  21.4 us (24%)
  starting transfers between devices  9.45 us (11%)
  waiting for transfers between devices  8.31 us (9%)
  local copies, waits for them, and re-layouts  1.74 us (2%)
    pallas_call x13, Pallas kernels, call(): pl.pallas_call(kernel, out_shape=outs, in_specs=[spec()] * len(args), out...  21.4 us
    all_to_all x1, blocking collectives, shards(): received = lax.all_to_all(summed, ('y', 'zh'), 0, 0)  21.2 us
    all_to_all x1, blocking collectives, shards(): row_levels = lax.all_to_all(spread, row_axes, 0, 0)  16 us
    all_to_all x1, blocking collectives, shards(): lax.all_to_all(spread, ('x', 'zl', 'c', 'zh'), 0, 0, axis_index_groups=me...  9.77 us
    ppermute x3, waiting for transfers between devices, along(): lax.ppermute(value, 'x', [(i, (i + by) % across_x) for i in range(across_...  7.24 us
    ppermute x3, starting transfers between devices, along(): lax.ppermute(value, 'x', [(i, (i + by) % across_x) for i in range(across_...  5.2 us
    ppermute x2, starting transfers between devices, traded(): return lax.ppermute(value, ('zl', 'c', 'zh'), trade)  4.08 us
  transfers between devices with their start and end apart: 7, of which 4 were waited for; matrix products, arithmetic and copies ran while one was open for 0% of the time, Pallas kernels for 11%

profile of v4, /device:TPU:0, one launch (start us, length us, event | category | flops | bytes accessed | tf_op | source)
XLA Modules:
  0.0 88.7 jit_solution(4764565593009814512)
XLA Ops:
  0.7 1.6 %collective-permute-start.1 = (f32[256,256]{1,0:T(8,128)}, f32[256,256]{1,0:T(8,128)S(1)}, u32[]{:S(2)}, u32[]{:S(2)}) collective-permute-start(f32[256,256]{1,0:T(8,128)} %refs_0_.1), channel_id=1, source_target_pairs={{0,32},{32,64},{64,96},{96,0},{1,33},{33,65},{65,97},{97,1},{2,34}... | collective-permute-start | bytes 786440 | tf_op jit(solution)/shard_map/ppermute | solution.py:302
  2.4 1.7 %collective-permute-start.2 = (f32[256,256]{1,0:T(8,128)}, f32[256,256]{1,0:T(8,128)S(1)}, u32[]{:S(2)}, u32[]{:S(2)}) collective-permute-start(f32[256,256]{1,0:T(8,128)} %refs_0_.1), channel_id=1, source_target_pairs={{0,96},{32,0},{64,32},{96,64},{1,97},{33,1},{65,33},{97,65},{2,98}... | collective-permute-start | bytes 786440 | tf_op jit(solution)/shard_map/ppermute | solution.py:302
  4.0 1.9 %collective-permute-start.3 = (f32[256,256]{1,0:T(8,128)}, f32[256,256]{1,0:T(8,128)S(1)}, u32[]{:S(2)}, u32[]{:S(2)}) collective-permute-start(f32[256,256]{1,0:T(8,128)} %refs_0_.1), channel_id=1, source_target_pairs={{0,64},{32,96},{64,0},{96,32},{1,65},{33,97},{65,1},{97,33},{2,66}... | collective-permute-start | bytes 786440 | tf_op jit(solution)/shard_map/ppermute | solution.py:302
  5.9 1.0 %copy-done = f32[256,256]{1,0:T(8,128)S(1)} copy-done((f32[256,256]{1,0:T(8,128)S(1)}, f32[256,256]{1,0:T(8,128)}, u32[]{:S(2)}) %copy-start) | copy-done | bytes 262168
  6.9 0.7 copy-done.3
  7.7 3.2 %collective-permute-done.1.refs_3_.refs_1_ = f32[256,256]{1,0:T(8,128)S(1)} collective-permute-done((f32[256,256]{1,0:T(8,128)}, f32[256,256]{1,0:T(8,128)S(1)}, u32[]{:S(2)}, u32[]{:S(2)}) %collective-permute-start.1) | collective-permute-done | bytes 262176 | tf_op jit(solution)/shard_map/ppermute | solution.py:302
  10.9 2.1 %collective-permute-start.4 = (f32[544,256]{1,0:T(8,128)S(1)}, f32[544,256]{1,0:T(8,128)S(1)}, u32[]{:S(2)}, u32[]{:S(2)}) collective-permute-start(f32[544,256]{1,0:T(8,128)S(1)} %pack.4), channel_id=1, source_target_pairs={{0,16},{1,17},{8,25},{9,24},{16,0},{17,1},{24,9},{25,8},{2,18},{3,... | collective-permute-start | bytes 1671176 | tf_op jit(solution)/shard_map/ppermute | solution.py:299
  13.0 0.5 split.2
  13.5 4.0 %collective-permute-done.3.refs_3_.refs_1_ = f32[256,256]{1,0:T(8,128)S(1)} collective-permute-done((f32[256,256]{1,0:T(8,128)}, f32[256,256]{1,0:T(8,128)S(1)}, u32[]{:S(2)}, u32[]{:S(2)}) %collective-permute-start.3) | collective-permute-done | bytes 262176 | tf_op jit(solution)/shard_map/ppermute | solution.py:302
  17.6 2.0 %collective-permute-start.5 = (f32[512,256]{1,0:T(8,128)S(1)}, f32[512,256]{1,0:T(8,128)S(1)}, u32[]{:S(2)}, u32[]{:S(2)}) collective-permute-start(f32[512,256]{1,0:T(8,128)S(1)} %pack.5), channel_id=1, source_target_pairs={{0,16},{1,17},{8,25},{9,24},{16,0},{17,1},{24,9},{25,8},{2,18},{3,... | collective-permute-start | bytes 1572872 | tf_op jit(solution)/shard_map/ppermute | solution.py:299
  19.6 0.3 split.3.refs_1_
  19.9 2.1 %score.4 = (f32[1024,512]{1,0:T(8,128)S(1)}, f32[1024,512]{1,0:T(8,128)S(1)}, bf16[512,256]{1,0:T(8,128)(2,1)S(1)}, f32[1024,128]{1,0:T(8,128)S(1)}, f32[1024,12...) custom-call(bf16[1024,768]{1,0:T(8,128)(2,1)S(1)} %get-tuple-element.39.refs_0_, ...), custom_call_target="tpu_custom_call" | custom-call | tf_op jit(solution)/shard_map/score/pallas_call | solution.py:269
  22.0 2.4 %score.5 = (f32[1024,512]{1,0:T(8,128)S(1)}, f32[1024,512]{1,0:T(8,128)S(1)}, bf16[512,256]{1,0:T(8,128)(2,1)S(1)}, f32[1024,128]{1,0:T(8,128)S(1)}, f32[1024,12...) custom-call(bf16[1024,768]{1,0:T(8,128)(2,1)S(1)} %get-tuple-element, ...), custom_call_target="tpu_custom_call", output_to_operand_aliasing={{3}: (5, {}), {4}: (6, {}), {5}: (7, {}), {6}: (8, {})} | custom-call | tf_op jit(solution)/shard_map/score/pallas_call | solution.py:269
  24.4 2.4 %score.6 = (f32[1024,512]{1,0:T(8,128)S(1)}, f32[1024,512]{1,0:T(8,128)S(1)}, bf16[512,256]{1,0:T(8,128)(2,1)S(1)}, f32[1024,128]{1,0:T(8,128)S(1)}, f32[1024,12...) custom-call(bf16[1024,768]{1,0:T(8,128)(2,1)S(1)} %get-tuple-element, ...), custom_call_target="tpu_custom_call", output_to_operand_aliasing={{3}: (5, {}), {4}: (6, {}), {5}: (7, {}), {6}: (8, {})} | custom-call | tf_op jit(solution)/shard_map/score/pallas_call | solution.py:269
  26.9 2.6 %score.7 = (f32[1024,512]{1,0:T(8,128)S(1)}, f32[1024,512]{1,0:T(8,128)S(1)}, bf16[512,256]{1,0:T(8,128)(2,1)S(1)}, f32[1024,128]{1,0:T(8,128)S(1)}, f32[1024,12...) custom-call(bf16[1024,768]{1,0:T(8,128)(2,1)S(1)} %get-tuple-element, ...), custom_call_target="tpu_custom_call", output_to_operand_aliasing={{3}: (5, {}), {4}: (6, {}), {5}: (7, {}), {6}: (8, {})} | custom-call | tf_op jit(solution)/shard_map/score/pallas_call | solution.py:269
  29.4 16.0 %all_to_all.15.refs_8_ = f32[16,2,8,128]{3,2,1,0:T(8,128)S(1)} all-to-all(f32[16,2,8,128]{3,2,1,0:T(8,128)S(1)} %broadcast_in_dim.4), channel_id=1, replica_groups=mesh['x'=4,'zl'=2,'c'=2,'y'=4,'zh'=2] {'c','y','zh'}, dimensions={0} | all-to-all | bytes 262144 | tf_op jit(solution)/shard_map/all_to_all | solution.py:371
  45.5 6.7 %columns.1 = (f32[8,256]{1,0:T(8,128)S(1)}, f32[1,128]{1,0:T(1,128)S(1)}, f32[1024,128]{1,0:T(8,128)S(1)}, f32[1024,128]{1,0:T(8,128)S(1)}) custom-call(f32[1024,512]{1,0:T(8,128)S(1)} %get-tuple-element.40.refs_0_, f32[1024,512]{1,0:T(8,128)S(1)} %get-tuple-element.48.refs_1_, f32[1024,512]{1,0:T(8,128)S(1)} %get-tuple-element.53.refs_2_, ...), custom_call_target="tpu_custom_call" | custom-call | tf_op jit(solution)/shard_map/columns/pallas_call | solution.py:269
  52.2 9.8 %all_to_all.16.refs_9_ = f32[8,8,256]{2,1,0:T(8,128)S(1)} all-to-all(f32[8,8,256]{2,1,0:T(8,128)S(1)} %broadcast_in_dim.5), channel_id=1, replica_groups={{0,16,32,48,64,80,96,112},{8,25,40,57,72,89,104,121},{1,17,33,49,65,81,..., dimensions={0} | all-to-all | bytes 131072 | tf_op jit(solution)/shard_map/all_to_all | solution.py:386
  62.0 1.8 %map_other.1 = f32[8,136,256]{2,1,0:T(8,128)S(1)} custom-call(f32[1024,512]{1,0:T(8,128)S(1)} %get-tuple-element.63.refs_4_.refs_0_, f32[1024,512]{1,0:T(8,128)S(1)} %get-tuple-element.64.refs_5_.refs_1_, f32[1024,512]{1,0:T(8,128)S(1)} %get-tuple-element.65.refs_6_.refs_2_, f32[1024,512]{1,0:T(8,128)S(1)} %get-tuple-element.66.refs_7_.refs_3_, ...), custom_call_target="tpu_custom_call" | custom-call | tf_op jit(solution)/shard_map/map_other/pallas_call | solution.py:269
  63.9 1.7 %map.1 = (f32[8,136,256]{2,1,0:T(8,128)S(1)}, f32[1,256]{1,0:T(1,128)S(1)}) custom-call(f32[1024,512]{1,0:T(8,128)S(1)} %get-tuple-element.40.refs_0_, f32[1024,512]{1,0:T(8,128)S(1)} %get-tuple-element.48.refs_1_, f32[1024,512]{1,0:T(8,128)S(1)} %get-tuple-element.53.refs_2_, f32[1024,512]{1,0:T(8,128)S(1)} %get-tuple-element.58.refs_3_, ...), custom_call_target="tpu_custom_call" | custom-call | tf_op jit(solution)/shard_map/map/pallas_call | solution.py:269
  65.6 1.0 %collective-permute-done.6 = f32[8,136,256]{2,1,0:T(8,128)S(1)} collective-permute-done((f32[8,136,256]{2,1,0:T(8,128)S(1)}, f32[8,136,256]{2,1,0:T(8,128)S(1)}, u32[]{:S(2)}, u32[]{:S(2)}) %collective-permute-start.6) | collective-permute-done | bytes 1114144 | tf_op jit(solution)/shard_map/ppermute | solution.py:305
  66.6 0.1 add.3
  66.8 21.2 %all_to_all.17.parts_ref = f32[8,136,256]{2,1,0:T(8,128)S(1)} all-to-all(f32[8,136,256]{2,1,0:T(8,128)S(1)} %add.3), channel_id=1, replica_groups=mesh['x'=4,'zl'=2,'c'=2,'y'=4,'zh'=2] {'y','zh'}, dimensions={0} | all-to-all | bytes 2228224 | tf_op jit(solution)/shard_map/all_to_all | solution.py:412
  88.0 0.8 quotient.1
  (19 shorter events, 0.4 us)
Async XLA Ops:
  0.6 19.0 %collective-permute-start = (f32[1024,256]{1,0:T(8,128)}, f32[1024,256]{1,0:T(8,128)S(1)}, u32[]{:S(2)}, u32[]{:S(2)}) collective-permute-start(f32[1024,256]{1,0:T(8,128)} %x_ref.1), channel_id=1, source_target_pairs={{0,8},{8,0},{1,9},{9,1},{2,10},{10,2},{3,11},{11,3},{4,12},{12,4},... | collective-permute-start | bytes 3145736 | tf_op jit(solution)/shard_map/ppermute | solution.py:305
  0.7 10.1 %collective-permute-start.1 = (f32[256,256]{1,0:T(8,128)}, f32[256,256]{1,0:T(8,128)S(1)}, u32[]{:S(2)}, u32[]{:S(2)}) collective-permute-start(f32[256,256]{1,0:T(8,128)} %refs_0_.1), channel_id=1, source_target_pairs={{0,32},{32,64},{64,96},{96,0},{1,33},{33,65},{65,97},{97,1},{2,34}... | collective-permute-start | bytes 786440 | tf_op jit(solution)/shard_map/ppermute | solution.py:302
  2.4 11.1 %collective-permute-start.2 = (f32[256,256]{1,0:T(8,128)}, f32[256,256]{1,0:T(8,128)S(1)}, u32[]{:S(2)}, u32[]{:S(2)}) collective-permute-start(f32[256,256]{1,0:T(8,128)} %refs_0_.1), channel_id=1, source_target_pairs={{0,96},{32,0},{64,32},{96,64},{1,97},{33,1},{65,33},{97,65},{2,98}... | collective-permute-start | bytes 786440 | tf_op jit(solution)/shard_map/ppermute | solution.py:302
  4.0 13.5 %collective-permute-start.3 = (f32[256,256]{1,0:T(8,128)}, f32[256,256]{1,0:T(8,128)S(1)}, u32[]{:S(2)}, u32[]{:S(2)}) collective-permute-start(f32[256,256]{1,0:T(8,128)} %refs_0_.1), channel_id=1, source_target_pairs={{0,64},{32,96},{64,0},{96,32},{1,65},{33,97},{65,1},{97,33},{2,66}... | collective-permute-start | bytes 786440 | tf_op jit(solution)/shard_map/ppermute | solution.py:302
  5.9 1.0 %copy-start = (f32[256,256]{1,0:T(8,128)S(1)}, f32[256,256]{1,0:T(8,128)}, u32[]{:S(2)}) copy-start(f32[256,256]{1,0:T(8,128)} %refs_0_.1) | copy-start | bytes 786436
  6.9 0.7 copy-start.3
  7.6 5.3 %copy-start.2 = (f32[1024,256]{1,0:T(8,128)S(1)}, f32[1024,256]{1,0:T(8,128)}, u32[]{:S(2)}) copy-start(f32[1024,256]{1,0:T(8,128)} %x_ref.1) | copy-start | bytes 3145732
  10.9 13.5 %collective-permute-start.4 = (f32[544,256]{1,0:T(8,128)S(1)}, f32[544,256]{1,0:T(8,128)S(1)}, u32[]{:S(2)}, u32[]{:S(2)}) collective-permute-start(f32[544,256]{1,0:T(8,128)S(1)} %pack.4), channel_id=1, source_target_pairs={{0,16},{1,17},{8,25},{9,24},{16,0},{17,1},{24,9},{25,8},{2,18},{3,... | collective-permute-start | bytes 1671176 | tf_op jit(solution)/shard_map/ppermute | solution.py:299
  13.5 6.4 %copy-start.1 = (f32[256,256]{1,0:T(8,128)S(1)}, f32[256,256]{1,0:T(8,128)}, u32[]{:S(2)}) copy-start(f32[256,256]{1,0:T(8,128)} %refs_0_.1) | copy-start | bytes 786436
  13.5 6.4 %copy-start.4 = (f32[4096]{0:T(1024)S(1)}, f32[4096]{0:T(1024)}, u32[]{:S(2)}) copy-start(f32[4096]{0:T(1024)} %param.5) | copy-start | bytes 49156
  17.6 9.3 %collective-permute-start.5 = (f32[512,256]{1,0:T(8,128)S(1)}, f32[512,256]{1,0:T(8,128)S(1)}, u32[]{:S(2)}, u32[]{:S(2)}) collective-permute-start(f32[512,256]{1,0:T(8,128)S(1)} %pack.5), channel_id=1, source_target_pairs={{0,16},{1,17},{8,25},{9,24},{16,0},{17,1},{24,9},{25,8},{2,18},{3,... | collective-permute-start | bytes 1572872 | tf_op jit(solution)/shard_map/ppermute | solution.py:299
  63.8 2.8 %collective-permute-start.6 = (f32[8,136,256]{2,1,0:T(8,128)S(1)}, f32[8,136,256]{2,1,0:T(8,128)S(1)}, u32[]{:S(2)}, u32[]{:S(2)}) collective-permute-start(f32[8,136,256]{2,1,0:T(8,128)S(1)} %map_other.1), channel_id=1, source_target_pairs={{0,8},{8,0},{1,9},{9,1},{2,10},{10,2},{3,11},{11,3},{4,12},{12,4},... | collective-permute-start | bytes 3342344 | tf_op jit(solution)/shard_map/ppermute | solution.py:305

commit v5 on v4

--- a/solution.py
+++ b/solution.py
@@ -139,8 +139,8 @@
     group = rows_ref.shape[0] // 2
     mine = lax.axis_index("y") * lax.axis_size("zh") + lax.axis_index("zh")
     for side in range(2):
-        parts = [rows_ref[half * group + k, side] for k in range(group)]
-        parts += [rows_ref[(1 - half) * group + k, 1 - side] for k in range(group)]
+        parts = [rows_ref[2 * k + half, side] for k in range(group)]
+        parts += [rows_ref[2 * k + 1 - half, 1 - side] for k in range(group)]
         add = log_targets - log_sum(parts)
         for k in range(add.shape[0]):
             add_refs[side][k * 128 : (k + 1) * 128, :] = jnp.broadcast_to(add[k : k + 1, :], (128, 128)).T
@@ -366,7 +366,7 @@
             rest = traded(rest)
             blocks[3] = [rest, rest]
     levels = result[7]
-    row_axes = ("c", "y", "zh")
+    row_axes = ("y", "zh", "c")
     spread = jnp.broadcast_to(levels[None], (2 * tgts,) + levels.shape)
     row_levels = lax.all_to_all(spread, row_axes, 0, 0)
     column_level, own_source, add, other_add = call(
@@ -382,7 +382,7 @@
     members = []
     for layer in range(2):
         for c in range(2):
-            members.append([((k * 2 + zl) * 2 + c) * 2 + (layer ^ (zl & c)) for k in range(across_x) for zl in range(2)])
+            members.append([((k * 2 + zl) * 2 + c) * 2 + (layer ^ (zl & c)) for zl in range(2) for k in range(across_x)])
     column_levels = lax.all_to_all(spread, ("x", "zl", "c", "zh"), 0, 0, axis_index_groups=members)
     scratch = [VMEM(column_level.shape, f32)]
     partial_out = VMEM((tgts, share + 8, width), f32)

time: 89 us -> 88.9 us (level)
  no operation moved by 1% of the time
where the time goes in v5:
time: 88.9 us; the launch traced here: 88.6 us
  blocking collectives  46.8 us (53%)
  Pallas kernels  21.4 us (24%)
  starting transfers between devices  9.45 us (11%)
  waiting for transfers between devices  8.31 us (9%)
  local copies, waits for them, and re-layouts  1.74 us (2%)
    pallas_call x13, Pallas kernels, call(): pl.pallas_call(kernel, out_shape=outs, in_specs=[spec()] * len(args), out...  21.4 us
    all_to_all x1, blocking collectives, shards(): received = lax.all_to_all(summed, ('y', 'zh'), 0, 0)  21.3 us
    all_to_all x1, blocking collectives, shards(): row_levels = lax.all_to_all(spread, row_axes, 0, 0)  15.7 us
    all_to_all x1, blocking collectives, shards(): lax.all_to_all(spread, ('x', 'zl', 'c', 'zh'), 0, 0, axis_index_groups=me...  9.85 us
    ppermute x3, waiting for transfers between devices, along(): lax.ppermute(value, 'x', [(i, (i + by) % across_x) for i in range(across_...  7.24 us
    ppermute x3, starting transfers between devices, along(): lax.ppermute(value, 'x', [(i, (i + by) % across_x) for i in range(across_...  5.2 us
    ppermute x2, starting transfers between devices, traded(): return lax.ppermute(value, ('zl', 'c', 'zh'), trade)  4.08 us
  transfers between devices with their start and end apart: 7, of which 4 were waited for; matrix products, arithmetic and copies ran while one was open for 0% of the time, Pallas kernels for 11%

profile of v5, /device:TPU:0, one launch (start us, length us, event | category | flops | bytes accessed | tf_op | source)
XLA Modules:
  0.0 88.6 jit_solution(9505241438243769088)
XLA Ops:
  0.7 1.6 %collective-permute-start.1 = (f32[256,256]{1,0:T(8,128)}, f32[256,256]{1,0:T(8,128)S(1)}, u32[]{:S(2)}, u32[]{:S(2)}) collective-permute-start(f32[256,256]{1,0:T(8,128)} %refs_0_.1), channel_id=1, source_target_pairs={{0,32},{32,64},{64,96},{96,0},{1,33},{33,65},{65,97},{97,1},{2,34}... | collective-permute-start | bytes 786440 | tf_op jit(solution)/shard_map/ppermute | solution.py:302
  2.4 1.7 %collective-permute-start.2 = (f32[256,256]{1,0:T(8,128)}, f32[256,256]{1,0:T(8,128)S(1)}, u32[]{:S(2)}, u32[]{:S(2)}) collective-permute-start(f32[256,256]{1,0:T(8,128)} %refs_0_.1), channel_id=1, source_target_pairs={{0,96},{32,0},{64,32},{96,64},{1,97},{33,1},{65,33},{97,65},{2,98}... | collective-permute-start | bytes 786440 | tf_op jit(solution)/shard_map/ppermute | solution.py:302
  4.0 1.9 %collective-permute-start.3 = (f32[256,256]{1,0:T(8,128)}, f32[256,256]{1,0:T(8,128)S(1)}, u32[]{:S(2)}, u32[]{:S(2)}) collective-permute-start(f32[256,256]{1,0:T(8,128)} %refs_0_.1), channel_id=1, source_target_pairs={{0,64},{32,96},{64,0},{96,32},{1,65},{33,97},{65,1},{97,33},{2,66}... | collective-permute-start | bytes 786440 | tf_op jit(solution)/shard_map/ppermute | solution.py:302
  5.9 1.0 %copy-done = f32[256,256]{1,0:T(8,128)S(1)} copy-done((f32[256,256]{1,0:T(8,128)S(1)}, f32[256,256]{1,0:T(8,128)}, u32[]{:S(2)}) %copy-start) | copy-done | bytes 262168
  6.9 0.7 copy-done.3
  7.7 3.2 %collective-permute-done.1.refs_3_.refs_1_ = f32[256,256]{1,0:T(8,128)S(1)} collective-permute-done((f32[256,256]{1,0:T(8,128)}, f32[256,256]{1,0:T(8,128)S(1)}, u32[]{:S(2)}, u32[]{:S(2)}) %collective-permute-start.1) | collective-permute-done | bytes 262176 | tf_op jit(solution)/shard_map/ppermute | solution.py:302
  10.9 2.1 %collective-permute-start.4 = (f32[544,256]{1,0:T(8,128)S(1)}, f32[544,256]{1,0:T(8,128)S(1)}, u32[]{:S(2)}, u32[]{:S(2)}) collective-permute-start(f32[544,256]{1,0:T(8,128)S(1)} %pack.4), channel_id=1, source_target_pairs={{0,16},{1,17},{8,25},{9,24},{16,0},{17,1},{24,9},{25,8},{2,18},{3,... | collective-permute-start | bytes 1671176 | tf_op jit(solution)/shard_map/ppermute | solution.py:299
  13.0 0.5 split.2
  13.5 4.0 %collective-permute-done.3.refs_3_.refs_1_ = f32[256,256]{1,0:T(8,128)S(1)} collective-permute-done((f32[256,256]{1,0:T(8,128)}, f32[256,256]{1,0:T(8,128)S(1)}, u32[]{:S(2)}, u32[]{:S(2)}) %collective-permute-start.3) | collective-permute-done | bytes 262176 | tf_op jit(solution)/shard_map/ppermute | solution.py:302
  17.6 2.0 %collective-permute-start.5 = (f32[512,256]{1,0:T(8,128)S(1)}, f32[512,256]{1,0:T(8,128)S(1)}, u32[]{:S(2)}, u32[]{:S(2)}) collective-permute-start(f32[512,256]{1,0:T(8,128)S(1)} %pack.5), channel_id=1, source_target_pairs={{0,16},{1,17},{8,25},{9,24},{16,0},{17,1},{24,9},{25,8},{2,18},{3,... | collective-permute-start | bytes 1572872 | tf_op jit(solution)/shard_map/ppermute | solution.py:299
  19.6 0.3 split.3.refs_1_
  19.9 2.1 %score.4 = (f32[1024,512]{1,0:T(8,128)S(1)}, f32[1024,512]{1,0:T(8,128)S(1)}, bf16[512,256]{1,0:T(8,128)(2,1)S(1)}, f32[1024,128]{1,0:T(8,128)S(1)}, f32[1024,12...) custom-call(bf16[1024,768]{1,0:T(8,128)(2,1)S(1)} %get-tuple-element.39.refs_0_, ...), custom_call_target="tpu_custom_call" | custom-call | tf_op jit(solution)/shard_map/score/pallas_call | solution.py:269
  22.0 2.4 %score.5 = (f32[1024,512]{1,0:T(8,128)S(1)}, f32[1024,512]{1,0:T(8,128)S(1)}, bf16[512,256]{1,0:T(8,128)(2,1)S(1)}, f32[1024,128]{1,0:T(8,128)S(1)}, f32[1024,12...) custom-call(bf16[1024,768]{1,0:T(8,128)(2,1)S(1)} %get-tuple-element, ...), custom_call_target="tpu_custom_call", output_to_operand_aliasing={{3}: (5, {}), {4}: (6, {}), {5}: (7, {}), {6}: (8, {})} | custom-call | tf_op jit(solution)/shard_map/score/pallas_call | solution.py:269
  24.4 2.4 %score.6 = (f32[1024,512]{1,0:T(8,128)S(1)}, f32[1024,512]{1,0:T(8,128)S(1)}, bf16[512,256]{1,0:T(8,128)(2,1)S(1)}, f32[1024,128]{1,0:T(8,128)S(1)}, f32[1024,12...) custom-call(bf16[1024,768]{1,0:T(8,128)(2,1)S(1)} %get-tuple-element, ...), custom_call_target="tpu_custom_call", output_to_operand_aliasing={{3}: (5, {}), {4}: (6, {}), {5}: (7, {}), {6}: (8, {})} | custom-call | tf_op jit(solution)/shard_map/score/pallas_call | solution.py:269
  26.9 2.6 %score.7 = (f32[1024,512]{1,0:T(8,128)S(1)}, f32[1024,512]{1,0:T(8,128)S(1)}, bf16[512,256]{1,0:T(8,128)(2,1)S(1)}, f32[1024,128]{1,0:T(8,128)S(1)}, f32[1024,12...) custom-call(bf16[1024,768]{1,0:T(8,128)(2,1)S(1)} %get-tuple-element, ...), custom_call_target="tpu_custom_call", output_to_operand_aliasing={{3}: (5, {}), {4}: (6, {}), {5}: (7, {}), {6}: (8, {})} | custom-call | tf_op jit(solution)/shard_map/score/pallas_call | solution.py:269
  29.4 15.7 %all_to_all.15.refs_8_ = f32[16,2,8,128]{3,2,1,0:T(8,128)S(1)} all-to-all(f32[16,2,8,128]{3,2,1,0:T(8,128)S(1)} %broadcast_in_dim.4), channel_id=1, replica_groups=mesh['x'=4,'zl'=2,'c'=2,'y'=4,'zh'=2] {'y','zh','c'}, dimensions={0} | all-to-all | bytes 262144 | tf_op jit(solution)/shard_map/all_to_all | solution.py:371
  45.1 6.7 %columns.1 = (f32[8,256]{1,0:T(8,128)S(1)}, f32[1,128]{1,0:T(1,128)S(1)}, f32[1024,128]{1,0:T(8,128)S(1)}, f32[1024,128]{1,0:T(8,128)S(1)}) custom-call(f32[1024,512]{1,0:T(8,128)S(1)} %get-tuple-element.40.refs_0_, f32[1024,512]{1,0:T(8,128)S(1)} %get-tuple-element.48.refs_1_, f32[1024,512]{1,0:T(8,128)S(1)} %get-tuple-element.53.refs_2_, ...), custom_call_target="tpu_custom_call" | custom-call | tf_op jit(solution)/shard_map/columns/pallas_call | solution.py:269
  51.8 9.9 %all_to_all.16.refs_9_ = f32[8,8,256]{2,1,0:T(8,128)S(1)} all-to-all(f32[8,8,256]{2,1,0:T(8,128)S(1)} %broadcast_in_dim.5), channel_id=1, replica_groups={{0,32,64,96,16,48,80,112},{8,40,72,104,25,57,89,121},{1,33,65,97,17,49,..., dimensions={0} | all-to-all | bytes 131072 | tf_op jit(solution)/shard_map/all_to_all | solution.py:386
  61.7 1.8 %map_other.1 = f32[8,136,256]{2,1,0:T(8,128)S(1)} custom-call(f32[1024,512]{1,0:T(8,128)S(1)} %get-tuple-element.63.refs_4_.refs_0_, f32[1024,512]{1,0:T(8,128)S(1)} %get-tuple-element.64.refs_5_.refs_1_, f32[1024,512]{1,0:T(8,128)S(1)} %get-tuple-element.65.refs_6_.refs_2_, f32[1024,512]{1,0:T(8,128)S(1)} %get-tuple-element.66.refs_7_.refs_3_, ...), custom_call_target="tpu_custom_call" | custom-call | tf_op jit(solution)/shard_map/map_other/pallas_call | solution.py:269
  63.6 1.7 %map.1 = (f32[8,136,256]{2,1,0:T(8,128)S(1)}, f32[1,256]{1,0:T(1,128)S(1)}) custom-call(f32[1024,512]{1,0:T(8,128)S(1)} %get-tuple-element.40.refs_0_, f32[1024,512]{1,0:T(8,128)S(1)} %get-tuple-element.48.refs_1_, f32[1024,512]{1,0:T(8,128)S(1)} %get-tuple-element.53.refs_2_, f32[1024,512]{1,0:T(8,128)S(1)} %get-tuple-element.58.refs_3_, ...), custom_call_target="tpu_custom_call" | custom-call | tf_op jit(solution)/shard_map/map/pallas_call | solution.py:269
  65.3 1.0 %collective-permute-done.6 = f32[8,136,256]{2,1,0:T(8,128)S(1)} collective-permute-done((f32[8,136,256]{2,1,0:T(8,128)S(1)}, f32[8,136,256]{2,1,0:T(8,128)S(1)}, u32[]{:S(2)}, u32[]{:S(2)}) %collective-permute-start.6) | collective-permute-done | bytes 1114144 | tf_op jit(solution)/shard_map/ppermute | solution.py:305
  66.3 0.1 add.3
  66.5 21.3 %all_to_all.17.parts_ref = f32[8,136,256]{2,1,0:T(8,128)S(1)} all-to-all(f32[8,136,256]{2,1,0:T(8,128)S(1)} %add.3), channel_id=1, replica_groups=mesh['x'=4,'zl'=2,'c'=2,'y'=4,'zh'=2] {'y','zh'}, dimensions={0} | all-to-all | bytes 2228224 | tf_op jit(solution)/shard_map/all_to_all | solution.py:412
  87.8 0.8 quotient.1
  (19 shorter events, 0.4 us)
Async XLA Ops:
  0.6 19.0 %collective-permute-start = (f32[1024,256]{1,0:T(8,128)}, f32[1024,256]{1,0:T(8,128)S(1)}, u32[]{:S(2)}, u32[]{:S(2)}) collective-permute-start(f32[1024,256]{1,0:T(8,128)} %x_ref.1), channel_id=1, source_target_pairs={{0,8},{8,0},{1,9},{9,1},{2,10},{10,2},{3,11},{11,3},{4,12},{12,4},... | collective-permute-start | bytes 3145736 | tf_op jit(solution)/shard_map/ppermute | solution.py:305
  0.7 10.1 %collective-permute-start.1 = (f32[256,256]{1,0:T(8,128)}, f32[256,256]{1,0:T(8,128)S(1)}, u32[]{:S(2)}, u32[]{:S(2)}) collective-permute-start(f32[256,256]{1,0:T(8,128)} %refs_0_.1), channel_id=1, source_target_pairs={{0,32},{32,64},{64,96},{96,0},{1,33},{33,65},{65,97},{97,1},{2,34}... | collective-permute-start | bytes 786440 | tf_op jit(solution)/shard_map/ppermute | solution.py:302
  2.4 11.1 %collective-permute-start.2 = (f32[256,256]{1,0:T(8,128)}, f32[256,256]{1,0:T(8,128)S(1)}, u32[]{:S(2)}, u32[]{:S(2)}) collective-permute-start(f32[256,256]{1,0:T(8,128)} %refs_0_.1), channel_id=1, source_target_pairs={{0,96},{32,0},{64,32},{96,64},{1,97},{33,1},{65,33},{97,65},{2,98}... | collective-permute-start | bytes 786440 | tf_op jit(solution)/shard_map/ppermute | solution.py:302
  4.0 13.5 %collective-permute-start.3 = (f32[256,256]{1,0:T(8,128)}, f32[256,256]{1,0:T(8,128)S(1)}, u32[]{:S(2)}, u32[]{:S(2)}) collective-permute-start(f32[256,256]{1,0:T(8,128)} %refs_0_.1), channel_id=1, source_target_pairs={{0,64},{32,96},{64,0},{96,32},{1,65},{33,97},{65,1},{97,33},{2,66}... | collective-permute-start | bytes 786440 | tf_op jit(solution)/shard_map/ppermute | solution.py:302
  5.9 1.0 %copy-start = (f32[256,256]{1,0:T(8,128)S(1)}, f32[256,256]{1,0:T(8,128)}, u32[]{:S(2)}) copy-start(f32[256,256]{1,0:T(8,128)} %refs_0_.1) | copy-start | bytes 786436
  6.9 0.7 copy-start.3
  7.6 5.3 %copy-start.2 = (f32[1024,256]{1,0:T(8,128)S(1)}, f32[1024,256]{1,0:T(8,128)}, u32[]{:S(2)}) copy-start(f32[1024,256]{1,0:T(8,128)} %x_ref.1) | copy-start | bytes 3145732
  10.9 13.5 %collective-permute-start.4 = (f32[544,256]{1,0:T(8,128)S(1)}, f32[544,256]{1,0:T(8,128)S(1)}, u32[]{:S(2)}, u32[]{:S(2)}) collective-permute-start(f32[544,256]{1,0:T(8,128)S(1)} %pack.4), channel_id=1, source_target_pairs={{0,16},{1,17},{8,25},{9,24},{16,0},{17,1},{24,9},{25,8},{2,18},{3,... | collective-permute-start | bytes 1671176 | tf_op jit(solution)/shard_map/ppermute | solution.py:299
  13.5 6.4 %copy-start.1 = (f32[256,256]{1,0:T(8,128)S(1)}, f32[256,256]{1,0:T(8,128)}, u32[]{:S(2)}) copy-start(f32[256,256]{1,0:T(8,128)} %refs_0_.1) | copy-start | bytes 786436
  13.5 6.4 %copy-start.4 = (f32[4096]{0:T(1024)S(1)}, f32[4096]{0:T(1024)}, u32[]{:S(2)}) copy-start(f32[4096]{0:T(1024)} %param.5) | copy-start | bytes 49156
  17.6 9.3 %collective-permute-start.5 = (f32[512,256]{1,0:T(8,128)S(1)}, f32[512,256]{1,0:T(8,128)S(1)}, u32[]{:S(2)}, u32[]{:S(2)}) collective-permute-start(f32[512,256]{1,0:T(8,128)S(1)} %pack.5), channel_id=1, source_target_pairs={{0,16},{1,17},{8,25},{9,24},{16,0},{17,1},{24,9},{25,8},{2,18},{3,... | collective-permute-start | bytes 1572872 | tf_op jit(solution)/shard_map/ppermute | solution.py:299
  63.5 2.8 %collective-permute-start.6 = (f32[8,136,256]{2,1,0:T(8,128)S(1)}, f32[8,136,256]{2,1,0:T(8,128)S(1)}, u32[]{:S(2)}, u32[]{:S(2)}) collective-permute-start(f32[8,136,256]{2,1,0:T(8,128)S(1)} %map_other.1), channel_id=1, source_target_pairs={{0,8},{8,0},{1,9},{9,1},{2,10},{10,2},{3,11},{11,3},{4,12},{12,4},... | collective-permute-start | bytes 3342344 | tf_op jit(solution)/shard_map/ppermute | solution.py:305
